TPU v7x, 32 devices: a whole 2x2x4 slice. The times are simulated.
32 devices in a mesh: dom: 8 (over z, x), feat: 4 (over y, core).
Axes of the slice: x: 2, y: 2, z: 4, core: 2. Of those that a mesh axis runs over, the one named last changes fastest.
Arguments:
- features: float32 [12288, 1024], P('dom', 'feat'), may hold values from -6 to 6
- degree: int32 [12288], P('dom'), may hold values from 1 to 9
- diag_adj: float32 [12288, 128], P('dom'), may hold values from -0.5 to 0.5
- remote_adj: float32 [8, 6, 128, 128], P('dom'), may hold values from -0.5 to 0.5
- read_block: int32 [8, 8], P('dom'), may hold values from 0 to 12, as said below
- tile_src: int32 [8, 6], P('dom'), may hold values from 0 to 7, as said below
- tile_row: int32 [8, 6], P('dom'), may hold values from 0 to 11, as said below
- w_first: float32 [1024, 1024], P('feat'), may hold values from -0.25 to 0.25
- b_first: float32 [1024], replicated, may hold values from -2 to 2
- w_second: float32 [1024, 1024], P('feat'), may hold values from -0.25 to 0.25
- b_second: float32 [1024], replicated, may hold values from -2 to 2
Outputs:
- embed: float32 [12288, 1024], P(('dom', 'feat'))
Inputs may be any that keep to these rules, and one draw needn't show every extreme that they name: `read_block`: entry [s, d] is the block of partition s that partition d reads, or 12 if d does not read s. Every partition reads exactly 3 other partitions, one block of each, and never itself. `tile_src`: tiles come in groups of 2 consecutive tiles with the same source partition; the sources of a partition's tiles are exactly the 3 partitions that it reads according to read_block. `tile_row`: within a group of 2 tiles with the same source, the block rows are distinct.
All inputs are finite; a program needn't handle non-finite values.
Results may differ from a plain program's by a relative error of at most 0.0003.
Values sent between devices are 32-bit elements; how exact they have to be, the bound alone decides.
No kernel may reach another device: no remote copies, remote signals or barrier semaphores. Data moves between devices by JAX's collectives and lax.ppermute only.
A program may use at most 128 MiB of HBM per device.

v0:
```python
import functools

import jax
import jax.numpy as jnp
from jax import lax
from jax.experimental import pallas as pl
from jax.experimental.pallas import tpu as pltpu
from jax.sharding import PartitionSpec as P

LANES = 128
TOUCH = 2
VMEM_LIMIT = 20 * 1024 * 1024
VMEM = pl.BlockSpec(memory_space=pltpu.VMEM)
SMEM = pl.BlockSpec(memory_space=pltpu.SMEM)
ANY = pl.BlockSpec(memory_space=pl.ANY)
PARAMS = pltpu.CompilerParams(vmem_limit_bytes=VMEM_LIMIT)


def dot(a, b):
    return jnp.dot(a, b, preferred_element_type=jnp.float32)


def dot3(a, b):
    return jnp.dot(a, b, precision=lax.Precision.HIGH, preferred_element_type=jnp.float32)


def halved(x):
    high = x.astype(jnp.bfloat16)
    return high, (x - high.astype(jnp.float32)).astype(jnp.bfloat16)


def f32(*dims):
    return jax.ShapeDtypeStruct(dims, jnp.float32)


def rows_at(index, height):
    return pl.ds(pl.multiple_of(index * height, height), height)


def scratch(*dims):
    return pltpu.VMEM(dims, jnp.float32)


def start_all(pairs, sems, first):
    copies = [pltpu.make_async_copy(a, b, sems.at[first + i]) for i, (a, b) in enumerate(pairs)]
    for copy in copies:
        copy.start()
    return copies


def wait_all(copies):
    for copy in copies:
        copy.wait()


def outgoing_body(want_ref, features, spread, blocks):
    chunk = spread.shape[1]
    for c in range(features.shape[1] // chunk):
        lanes = pl.ds(c * chunk, chunk)
        blocks[0, :, lanes] = features[:, lanes] * spread[...]


def outgoing_blocks(want, features, spread, tile):
    cols, chunk = features.shape[1], spread.shape[1]
    count = want.shape[0]
    return pl.pallas_call(
        outgoing_body,
        out_shape=f32(count, tile, cols),
        grid_spec=pltpu.PrefetchScalarGridSpec(
            num_scalar_prefetch=1,
            grid=(count,),
            in_specs=[
                pl.BlockSpec((tile, cols), lambda d, want: (want[d], 0)),
                pl.BlockSpec((tile, chunk), lambda d, want: (want[d], 0)),
            ],
            out_specs=pl.BlockSpec((1, tile, cols), lambda d, want: (d, 0, 0)),
        ),
        compiler_params=PARAMS,
    )(want, features, spread)


def partial_body(count, place_ref, *refs):
    lefts, rights, outs = refs[:count], refs[count : 2 * count], refs[2 * count :]
    left = jnp.concatenate([x[...] for x in lefts], axis=1)
    right = jnp.concatenate([w[...] for w in rights], axis=0)
    result = dot3(left, right)
    width = outs[0].shape[1]
    for c, out in enumerate(outs):
        out[...] = result[:, c * width : (c + 1) * width]


def partial_sums(place, at, lefts, weights, step, pieces):
    rows, cols = lefts[0].shape
    depth = weights[0].shape[0]
    count = len(lefts)
    width = cols // pieces
    return pl.pallas_call(
        functools.partial(partial_body, count),
        out_shape=[f32(rows, width)] * pieces,
        grid_spec=pltpu.PrefetchScalarGridSpec(
            num_scalar_prefetch=1,
            grid=(rows // step,),
            in_specs=[pl.BlockSpec((step, cols), lambda i, place: (i, 0))] * count
            + [pl.BlockSpec((depth, cols), lambda i, place: (0, place[at]))] * count,
            out_specs=[pl.BlockSpec((step, width), lambda i, place: (i, 0))] * pieces,
        ),
        compiler_params=PARAMS,
        cost_estimate=pl.CostEstimate(
            flops=6 * rows * depth * cols * count,
            bytes_accessed=4 * (count + 1) * rows * cols,
            transcendentals=0,
        ),
    )(place, *lefts, *weights)


def chosen_body(source_ref, incoming, chosen, sems):
    tile = incoming.shape[1]
    groups = chosen.shape[0] // tile
    wait_all(
        start_all(
            [(incoming.at[source_ref[TOUCH * g]], chosen.at[pl.ds(g * tile, tile)]) for g in range(groups)],
            sems,
            0,
        )
    )


def chosen_blocks(source, incoming):
    tile, cols = incoming.shape[1:]
    groups = source.shape[0] // TOUCH
    return pl.pallas_call(
        chosen_body,
        out_shape=f32(groups * tile, cols),
        in_specs=[SMEM, ANY],
        out_specs=ANY,
        scratch_shapes=[pltpu.SemaphoreType.DMA((groups,))],
        compiler_params=PARAMS,
    )(source, incoming)


def own_body(diag, spread, *refs):
    sums, base = refs[:-1], refs[-1]
    tile = diag.shape[1]
    for i in range(diag.shape[0] // tile):
        rows = pl.ds(i * tile, tile)
        total = sums[0][rows, :]
        for extra in sums[1:]:
            total = total + extra[rows, :]
        base[rows, :] = dot3(diag[rows, :], total * spread[rows, :])


def own_part(diag, spread, sums, c, step):
    rows, tile = diag.shape
    chunk = spread.shape[1]
    return pl.pallas_call(
        own_body,
        out_shape=f32(rows, chunk),
        grid=(rows // step,),
        in_specs=[pl.BlockSpec((step, tile), lambda i: (i, 0)), pl.BlockSpec((step, chunk), lambda i: (i, 0))]
        + [pl.BlockSpec((step, chunk), lambda i: (i, c))] * len(sums),
        out_specs=pl.BlockSpec((step, chunk), lambda i: (i, 0)),
        compiler_params=PARAMS,
    )(diag, spread, *sums)


def hidden_body(count, offset, row_ref, want_ref, first_ref, bias, base, remote, spread, diag, *refs):
    sums, (blocks, base_out), refs = refs[:count], refs[count : count + 2], refs[count + 2 :]
    sums_in, (total, remote_in, spread_in, diag_in, scaled, sems) = refs[:count], refs[count:]
    tiles, tile = remote.shape[:2]
    parts = blocks.shape[0]
    chunk = total.shape[1]
    early = start_all(
        list(zip(sums, sums_in)) + [(remote, remote_in), (base, total), (spread, spread_in), (diag, diag_in)],
        sems,
        0,
    )
    wait_all(early[: count + 2])
    for g in range(tiles // TOUCH):
        rows = pl.ds(g * tile, tile)
        block = sums_in[0][rows, :]
        for extra in sums_in[1:]:
            block = block + extra[rows, :]
        for k in range(TOUCH * g, TOUCH * g + TOUCH):
            total[rows_at(row_ref[k], tile), :] += dot3(remote_in[k], block)
    lanes = pl.ds(pl.multiple_of(first_ref[0] + offset, chunk), chunk)
    shift = bias[:, lanes]
    wait_all(early[count + 2 :])
    scaled[...] = jnp.maximum(total[...] * spread_in[...] + shift, 0.0) * spread_in[...]
    copies = start_all(
        [(scaled.at[rows_at(want_ref[d], tile)], blocks.at[d]) for d in range(parts)], sems, count + 4
    )
    for i in range(diag.shape[0] // tile):
        rows = pl.ds(i * tile, tile)
        total[rows, :] = dot3(diag_in[rows, :], scaled[rows, :])
    copies += start_all([(total, base_out)], sems, count + 4 + parts)
    wait_all(copies)


def hidden_blocks(row, want, first, offset, bias, base, remote, spread, diag, sums):
    rows, chunk = base.shape
    tile = diag.shape[1]
    parts = want.shape[0]
    count = len(sums)
    return pl.pallas_call(
        functools.partial(hidden_body, count, offset),
        out_shape=[f32(parts, tile, chunk), f32(rows, chunk)],
        in_specs=[SMEM] * 3 + [VMEM] + [ANY] * (4 + count),
        out_specs=[ANY, ANY],
        scratch_shapes=[scratch(*s.shape) for s in sums]
        + [scratch(*a.shape) for a in (base, remote, spread, diag, base)]
        + [pltpu.SemaphoreType.DMA((count + 5 + parts,))],
        compiler_params=PARAMS,
    )(row, want, first, bias, base, remote, spread, diag, *sums)


def pieces_body(source_ref, row_ref, place_ref, base, remote, spread, incoming, *refs):
    pieces, (total, remote_in, spread_in, incoming_in, sems) = refs[:-5], refs[-5:]
    tiles, tile = remote.shape[:2]
    early = start_all(
        [(incoming, incoming_in), (remote, remote_in), (base, total), (spread, spread_in)], sems, 0
    )
    wait_all(early[:3])
    for k in range(tiles):
        total[rows_at(row_ref[k], tile), :] += dot3(remote_in[k], incoming_in[source_ref[k]])
    wait_all(early[3:])
    total[...] = total[...] * spread_in[...]
    height = pieces[0].shape[0]
    wait_all(
        start_all([(total.at[rows_at(place_ref[j], height)], p) for j, p in enumerate(pieces)], sems, 4)
    )


def feature_pieces(source, row, place, base, remote, spread, incoming):
    rows, chunk = base.shape
    feats = place.shape[0]
    return pl.pallas_call(
        pieces_body,
        out_shape=[f32(rows // feats, chunk)] * feats,
        in_specs=[SMEM] * 3 + [ANY] * 4,
        out_specs=[ANY] * feats,
        scratch_shapes=[scratch(*a.shape) for a in (base, remote, spread, incoming)]
        + [pltpu.SemaphoreType.DMA((4 + feats,))],
        compiler_params=PARAMS,
    )(source, row, place, base, remote, spread, incoming)


def product_body(count, start, *refs):
    pieces, weights, (out, high, low) = refs[:count], refs[count : 2 * count], refs[2 * count :]
    chunk = pieces[0].shape[1]

    @pl.when(pl.program_id(0) == 0)
    def _():
        for j, piece in enumerate(pieces):
            lanes = pl.ds(j * chunk, chunk)
            high[:, lanes], low[:, lanes] = halved(piece[...])

    w_high, w_low = halved(jnp.concatenate([w[...] for w in weights], axis=0))
    product = dot(high[...], w_high) + (dot(high[...], w_low) + dot(low[...], w_high))
    out[...] = start[...] + product


def add_product(start, pieces, weights):
    rows, chunk = pieces[0].shape
    width = weights[0][0].shape[1]
    step = min(2 * LANES, width)
    count = len(pieces)
    return pl.pallas_call(
        functools.partial(product_body, count),
        out_shape=f32(rows, width),
        grid=(width // step,),
        in_specs=[pl.BlockSpec((start.shape[0], step), lambda j: (0, j))]
        + [pl.BlockSpec((rows, chunk), lambda j: (0, 0))] * count
        + [pl.BlockSpec((chunk, step), lambda j, c=c: (c, j)) for _, c in weights],
        out_specs=pl.BlockSpec((rows, step), lambda j: (0, j)),
        scratch_shapes=[pltpu.VMEM((rows, count * chunk), jnp.bfloat16)] * 2,
        compiler_params=PARAMS,
        cost_estimate=pl.CostEstimate(
            flops=6 * count * rows * chunk * width,
            bytes_accessed=4 * count * chunk * (rows + width) + 8 * rows * width,
            transcendentals=0,
        ),
    )(start, *pieces, *[w for w, _ in weights])


def solution(mesh):
    parts = mesh.shape["dom"]
    feats = mesh.shape["feat"]
    sides = 2 if feats % 2 == 0 else 1
    halves = feats // sides

    def feat_target(f, dh, dl):
        return (f // sides + dh) % halves * sides + (f % sides + dl) % sides

    def feat_send(x, dh, dl):
        return lax.ppermute(x, "feat", [(f, feat_target(f, dh, dl)) for f in range(feats)])

    def dom_exchange(x):
        return lax.all_to_all(x, "dom", split_axis=0, concat_axis=0, tiled=True)

    def per_device(
        features,
        degree,
        diag_adj,
        remote_adj,
        read_block,
        tile_src,
        tile_row,
        w_first,
        b_first,
        w_second,
        b_second,
    ):
        part, cols = features.shape
        tile = diag_adj.shape[1]
        blocks = part // tile
        remote = remote_adj[0]
        chunk = LANES if cols % LANES == 0 else cols
        chunks = cols // chunk
        f = lax.axis_index("feat")
        source, row = tile_src[0], tile_row[0]
        want = jnp.minimum(read_block[0], blocks - 1)
        shifts = [(dh, dl) for dh in range(halves) for dl in range(sides)]
        place = jnp.stack([jnp.asarray(feat_target(f, dh, dl), jnp.int32) for dh, dl in shifts])
        first = jnp.reshape(jnp.asarray(f * cols, jnp.int32), (1,))
        others = list(range(1, halves))
        piece = part // feats

        x_all = [features] + [feat_send(features, 0, dl) for dl in range(1, sides)]
        w_all = [w_first] + [feat_send(w_first, 0, dl) for dl in range(1, sides)]
        scaling = lax.rsqrt(degree.astype(jnp.float32))
        spread = jnp.broadcast_to(scaling[:, None], (part, chunk))
        outgoing = outgoing_blocks(want, features, spread, tile)

        sends = [partial_sums(place, dh * sides, x_all, w_all, 2 * tile, 1)[0] for dh in others]
        outgoing, sends = lax.optimization_barrier((outgoing, sends))
        incoming = dom_exchange(outgoing)
        sums = [partial_sums(place, 0, x_all, w_all, 2 * tile, 1)[0]]
        sums += [feat_send(x, dh, 0) for dh, x in zip(others, sends)]

        chosen = chosen_blocks(source, incoming)
        chosen_all = [chosen] + [feat_send(chosen, 0, dl) for dl in range(1, sides)]
        height = chosen.shape[0]
        remote_sends = [partial_sums(place, dh * sides, chosen_all, w_all, height, chunks) for dh in others]
        remote_own = partial_sums(place, 0, chosen_all, w_all, height, chunks)
        remote_sums = [
            [remote_own[c]] + [feat_send(x[c], dh, 0) for dh, x in zip(others, remote_sends)]
            for c in range(chunks)
        ]

        shares = chunks if parts % chunks == 0 else 1
        share = lax.axis_index("dom") % shares
        share_rows = w_second.shape[0] // shares

        def share_send(x, k):
            pairs = [(s, s // shares * shares + (s % shares + k) % shares) for s in range(parts)]
            return lax.ppermute(x, "dom", pairs)

        w2_sent = lax.dynamic_slice_in_dim(w_second, share * share_rows, share_rows, 0)
        w2_sent, _ = lax.optimization_barrier((w2_sent, [s[1:] for s in remote_sums]))
        w2_got = [feat_send(w2_sent, dh, 0) for dh in others]

        base = [own_part(diag_adj, spread, sums, c, piece) for c in range(chunks)]
        bias = b_first[None, :]
        collected = []
        outgoing = None
        for c in range(chunks):
            if c > 0:
                base[c], outgoing = lax.optimization_barrier((base[c], outgoing))
            outgoing, base_next = hidden_blocks(
                row, want, first, c * chunk, bias, base[c], remote, spread, diag_adj, remote_sums[c]
            )
            incoming = dom_exchange(outgoing)
            pieces = feature_pieces(source, row, place, base_next, remote, spread, incoming)
            collected.append(
                [p if dh == 0 and dl == 0 else feat_send(p, dh, dl) for (dh, dl), p in zip(shifts, pieces)]
            )

        w2_groups = [[got] + [share_send(got, k) for k in range(1, shares)] for got in w2_got]
        w2_core = [w_second] + [feat_send(w_second, 0, dl) for dl in range(1, sides)]
        out = b_second[None, :]
        for c in range(chunks):
            weights = [(w, c) for w in w2_core]
            for group in w2_groups:
                if shares == 1:
                    block = group[0][c * chunk : (c + 1) * chunk]
                else:
                    block = lax.select_n((share - c) % shares, *group)
                weights += [(block, 0)] + [(feat_send(block, 0, dl), 0) for dl in range(1, sides)]
            out = add_product(out, collected[c], weights)
        return out

    return jax.shard_map(
        per_device,
        mesh=mesh,
        in_specs=(
            P("dom", "feat"),
            P("dom"),
            P("dom", None),
            P("dom", None, None, None),
            P("dom", None),
            P("dom", None),
            P("dom", None),
            P("feat", None),
            P(),
            P("feat", None),
            P(),
        ),
        out_specs=P(("dom", "feat"), None),
        check_vma=False,
    )
```

profile of v0, /device:TPU:0, one launch (start us, length us, event | category | flops | bytes accessed | tf_op | source)
XLA Modules:
  0.0 133.7 jit_solution(1866417892511613300)
XLA Ops:
  2.2 1.4 %copy-done.1 = f32[1536,256]{1,0:T(8,128)S(1)} copy-done((f32[1536,256]{1,0:T(8,128)S(1)}, f32[1536,256]{1,0:T(8,128)}, u32[]{:S(2)}) %copy-start.1) | copy-done | bytes 1572888
  5.4 5.1 %shard_map.111 = f32[1536,256]{1,0:T(8,128)S(1)} custom-call(s32[4]{0:T(128)S(1)} %pad_add_fusion.place_ref, f32[1536,256]{1,0:T(8,128)S(1)} %copy-done.2, f32[1536,256]{1,0:T(8,128)} %collective-permute-done.refs_1_, f32[256,1024]{1,0:T(8,128)S(1)} %copy-done, f32[256,1024]{1,0:T(8,128)S(1)} %collective-permute-done.1.refs_3_), custom_call_target="tpu_custom_call" | custom-call | flops 1207959552 | bytes 4718592 | tf_op jit(solution)/shard_map/pallas_call | solution.py:97
  10.5 1.1 copy-done.15
  11.6 7.4 %all-to-all-start = ((f32[8,128,256]{2,1,0:T(8,128)}), f32[8,128,256]{2,1,0:T(8,128)}, u32[]{:S(2)}, u32[]{:S(2)}) async-start(f32[8,128,256]{2,1,0:T(8,128)} %copy-done.12), calls=%async_computation | async-start | bytes 2097152 | tf_op jit(solution)/shard_map/all_to_all | solution.py:298
  19.0 1.5 %collective-permute-start.2 = (f32[1536,256]{1,0:T(8,128)}, f32[1536,256]{1,0:T(8,128)}, u32[]{:S(2)}, u32[]{:S(2)}) collective-permute-start(f32[1536,256]{1,0:T(8,128)} %copy-done.15), channel_id=1, source_target_pairs={{0,2},{1,3},{2,0},{3,1},{4,6},{5,7},{6,4},{7,5},{8,10},{9,11},{10,... | collective-permute-start | bytes 4718600 | tf_op jit(solution)/shard_map/ppermute | solution.py:295
  20.5 24.5 %all-to-all-done.incoming = f32[8,128,256]{2,1,0:T(8,128)} async-done(((f32[8,128,256]{2,1,0:T(8,128)}), f32[8,128,256]{2,1,0:T(8,128)}, u32[]{:S(2)}, u32[]{:S(2)}) %all-to-all-start) | async-done | bytes 1048608 | tf_op jit(solution)/shard_map/all_to_all | solution.py:298
  45.1 1.6 %shard_map.113.refs_0_ = f32[384,256]{1,0:T(8,128)S(1)} custom-call(s32[6]{0:T(128)S(1)} %bitcast.22, f32[8,128,256]{2,1,0:T(8,128)} %all-to-all-done.incoming), custom_call_target="tpu_custom_call" | custom-call | tf_op jit(solution)/shard_map/pallas_call | solution.py:131
  46.7 1.7 %collective-permute-done.3.refs_1_ = f32[384,256]{1,0:T(8,128)S(1)} collective-permute-done((f32[384,256]{1,0:T(8,128)S(1)}, f32[384,256]{1,0:T(8,128)S(1)}, u32[]{:S(2)}, u32[]{:S(2)}) %collective-permute-start.3) | collective-permute-done | bytes 393248 | tf_op jit(solution)/shard_map/ppermute | solution.py:295
  48.5 1.7 %shard_map.115 = (f32[384,128]{1,0:T(8,128)}, f32[384,128]{1,0:T(8,128)S(1)}) custom-call(s32[4]{0:T(128)S(1)} %pad_add_fusion.place_ref, f32[384,256]{1,0:T(8,128)S(1)} %shard_map.113.refs_0_, f32[384,256]{1,0:T(8,128)S(1)} %collective-permute-done.3.refs_1_, f32[256,1024]{1,0:T(8,128)S(1)} %copy-done, f32[256,1024]{1,0:T(8,128)S(1)} %collective-permute-done.1.refs_3_), custom_call_target="tpu_custom_call" | custom-call | flops 301989888 | bytes 1179648 | tf_op jit(solution)/shard_map/pallas_call | solution.py:97
  51.6 1.5 %collective-permute-start.4 = (f32[384,128]{1,0:T(8,128)}, f32[384,128]{1,0:T(8,128)S(1)}, u32[]{:S(2)}, u32[]{:S(2)}) collective-permute-start(f32[384,128]{1,0:T(8,128)} %get-tuple-element.28), channel_id=1, source_target_pairs={{0,2},{1,3},{2,0},{3,1},{4,6},{5,7},{6,4},{7,5},{8,10},{9,11},{10,... | collective-permute-start | bytes 589832 | tf_op jit(solution)/shard_map/ppermute | solution.py:295
  53.6 1.4 %copy-done.3 = f32[1536,256]{1,0:T(8,128)S(1)} copy-done((f32[1536,256]{1,0:T(8,128)S(1)}, f32[1536,256]{1,0:T(8,128)}, u32[]{:S(2)}) %copy-start.3) | copy-done | bytes 1572888
  55.0 5.1 %shard_map.109.refs_0_ = f32[1536,256]{1,0:T(8,128)S(1)} custom-call(s32[4]{0:T(128)S(1)} %pad_add_fusion.place_ref, f32[1536,256]{1,0:T(8,128)S(1)} %copy-done.3, f32[1536,256]{1,0:T(8,128)} %collective-permute-done.refs_1_, f32[256,1024]{1,0:T(8,128)S(1)} %copy-done, f32[256,1024]{1,0:T(8,128)S(1)} %collective-permute-done.1.refs_3_), custom_call_target="tpu_custom_call" | custom-call | flops 1207959552 | bytes 4718592 | tf_op jit(solution)/shard_map/pallas_call | solution.py:97
  60.1 3.1 %shard_map.112.base = f32[1536,128]{1,0:T(8,128)S(1)} custom-call(f32[1536,128]{1,0:T(8,128)S(1)} %copy-done.6, f32[1536,128]{1,0:T(8,128)S(1)} %broadcast_in_dim.14.spread, f32[1536,256]{1,0:T(8,128)S(1)} %shard_map.109.refs_0_, f32[1536,256]{1,0:T(8,128)} %collective-permute-done.2.refs_1_), custom_call_target="tpu_custom_call" | custom-call | tf_op jit(solution)/shard_map/pallas_call | solution.py:155
  64.4 3.2 %shard_map.116 = (f32[8,128,128]{2,1,0:T(8,128)S(1)}, f32[1536,128]{1,0:T(8,128)S(1)}) custom-call(s32[6]{0:T(128)S(1)} %bitcast.18, s32[8]{0:T(128)S(1)} %minimum_bitcast_fusion.want_ref, s32[1]{0:T(128)} %bitcast.8.first_ref, f32[1,1024]{1,0:T(1,128)S(1)} %bitcast.16, f32[1536,128]{1,0:T(8,128)S(1)} %shard_map.112.base, f32[6,128,128]{2,1,0:T(8,128)S(1)} %bitcast.12, ...), custom_call_target="tpu_custom_call" | custom-call | tf_op jit(solution)/shard_map/pallas_call | solution.py:204
  69.3 4.3 %all-to-all-start.1 = ((f32[8,128,128]{2,1,0:T(8,128)}), f32[8,128,128]{2,1,0:T(8,128)}, u32[]{:S(2)}, u32[]{:S(2)}) async-start(f32[8,128,128]{2,1,0:T(8,128)} %copy-done.20), calls=%async_computation.1 | async-start | bytes 1048576 | tf_op jit(solution)/shard_map/all_to_all | solution.py:298
  74.7 1.6 %collective-permute-start.10 = (f32[128,1024]{1,0:T(8,128)S(1)}, f32[128,1024]{1,0:T(8,128)}, u32[]{:S(2)}, u32[]{:S(2)}) collective-permute-start(f32[128,1024]{1,0:T(8,128)S(1)} %constant_dynamic-slice_fusion), channel_id=1, source_target_pairs={{0,2},{1,3},{2,0},{3,1},{4,6},{5,7},{6,4},{7,5},{8,10},{9,11},{10,... | collective-permute-start | bytes 1572872 | tf_op jit(solution)/shard_map/ppermute | solution.py:295
  76.3 12.0 %collective-permute-done.10 = f32[128,1024]{1,0:T(8,128)} collective-permute-done((f32[128,1024]{1,0:T(8,128)S(1)}, f32[128,1024]{1,0:T(8,128)}, u32[]{:S(2)}, u32[]{:S(2)}) %collective-permute-start.10) | collective-permute-done | bytes 524320 | tf_op jit(solution)/shard_map/ppermute | solution.py:295
  88.3 1.6 %collective-permute-start.11 = (f32[128,1024]{1,0:T(8,128)}, f32[128,1024]{1,0:T(8,128)}, u32[]{:S(2)}, u32[]{:S(2)}) collective-permute-start(f32[128,1024]{1,0:T(8,128)} %collective-permute-done.10), channel_id=1, source_target_pairs={{0,4},{4,0},{8,12},{12,8},{16,20},{20,16},{24,28},{28,24},{1,5},{5... | collective-permute-start | bytes 1572872 | tf_op jit(solution)/shard_map/ppermute | solution.py:356
  89.9 2.7 %shard_map.119.base = f32[1536,128]{1,0:T(8,128)S(1)} custom-call(f32[1536,128]{1,0:T(8,128)S(1)} %copy-done.7, f32[1536,128]{1,0:T(8,128)S(1)} %broadcast_in_dim.14.spread, f32[1536,256]{1,0:T(8,128)S(1)} %copy-done.5, f32[1536,256]{1,0:T(8,128)} %collective-permute-done.2.refs_1_), custom_call_target="tpu_custom_call" | custom-call | tf_op jit(solution)/shard_map/pallas_call | solution.py:155
  92.6 3.3 %shard_map.120 = (f32[8,128,128]{2,1,0:T(8,128)}, f32[1536,128]{1,0:T(8,128)S(1)}) custom-call(s32[6]{0:T(128)S(1)} %bitcast.19, s32[8]{0:T(128)S(1)} %minimum_bitcast_fusion.want_ref, s32[1]{0:T(128)} %bitcast.8.first_ref, f32[1,1024]{1,0:T(1,128)S(1)} %bitcast.17, f32[1536,128]{1,0:T(8,128)S(1)} %shard_map.119.base, f32[6,128,128]{2,1,0:T(8,128)S(1)} %bitcast.13, ...), custom_call_target="tpu_custom_call" | custom-call | tf_op jit(solution)/shard_map/pallas_call | solution.py:204
  96.8 4.7 %all-to-all-start.2 = ((f32[8,128,128]{2,1,0:T(8,128)}), f32[8,128,128]{2,1,0:T(8,128)S(1)}, u32[]{:S(2)}, u32[]{:S(2)}) async-start(f32[8,128,128]{2,1,0:T(8,128)} %get-tuple-element.40), calls=%async_computation.2 | async-start | bytes 1048576 | tf_op jit(solution)/shard_map/all_to_all | solution.py:298
  101.6 2.3 %broadcast_select_fusion = (f32[128,1024]{1,0:T(8,128)}, f32[128,1024]{1,0:T(8,128)}) fusion(f32[128,1024]{1,0:T(8,128)} %collective-permute-done.10, f32[128,1024]{1,0:T(8,128)} %collective-permute-done.11, pred[]{:T(512)S(6)} %select_n.90, pred[]{:T(512)S(6)} %select_n.85), kind=kLoop, calls=%fused_computation | loop fusion | flops 262144 | bytes 2097154 | tf_op jit(solution)/shard_map/select_n | solution.py:387
  104.4 3.1 %shard_map.117 = (f32[384,128]{1,0:T(8,128)S(1)}, f32[384,128]{1,0:T(8,128)}, f32[384,128]{1,0:T(8,128)}, f32[384,128]{1,0:T(8,128)}) custom-call(s32[6]{0:T(128)S(1)} %bitcast.23, s32[6]{0:T(128)S(1)} %bitcast.20, s32[4]{0:T(128)S(1)} %pad_add_fusion.place_ref, f32[1536,128]{1,0:T(8,128)S(1)} %copy-done.17, f32[6,128,128]{2,1,0:T(8,128)S(1)} %bitcast.14, ...), custom_call_target="tpu_custom_call" | custom-call | tf_op jit(solution)/shard_map/pallas_call | solution.py:236
  108.2 1.5 %collective-permute-start.6 = (f32[384,128]{1,0:T(8,128)}, f32[384,128]{1,0:T(8,128)}, u32[]{:S(2)}, u32[]{:S(2)}) collective-permute-start(f32[384,128]{1,0:T(8,128)} %get-tuple-element.33), channel_id=1, source_target_pairs={{0,2},{1,3},{2,0},{3,1},{4,6},{5,7},{6,4},{7,5},{8,10},{9,11},{10,... | collective-permute-start | bytes 589832 | tf_op jit(solution)/shard_map/ppermute | solution.py:295
  110.1 4.3 %all-to-all-done.2.incoming = f32[8,128,128]{2,1,0:T(8,128)S(1)} async-done(((f32[8,128,128]{2,1,0:T(8,128)}), f32[8,128,128]{2,1,0:T(8,128)S(1)}, u32[]{:S(2)}, u32[]{:S(2)}) %all-to-all-start.2) | async-done | bytes 524320 | tf_op jit(solution)/shard_map/all_to_all | solution.py:298
  114.3 1.1 copy-done.19
  115.5 2.4 %shard_map.121 = (f32[384,128]{1,0:T(8,128)S(1)}, f32[384,128]{1,0:T(8,128)S(1)}, f32[384,128]{1,0:T(8,128)S(1)}, f32[384,128]{1,0:T(8,128)S(1)}) custom-call(s32[6]{0:T(128)S(1)} %bitcast.24, s32[6]{0:T(128)S(1)} %bitcast.21, s32[4]{0:T(128)S(1)} %pad_add_fusion.place_ref, f32[1536,128]{1,0:T(8,128)S(1)} %copy-done.19, f32[6,128,128]{2,1,0:T(8,128)S(1)} %bitcast.15, ...), custom_call_target="tpu_custom_call" | custom-call | tf_op jit(solution)/shard_map/pallas_call | solution.py:236
  118.0 1.6 %collective-permute-start.14 = (f32[384,128]{1,0:T(8,128)S(1)}, f32[384,128]{1,0:T(8,128)S(1)}, u32[]{:S(2)}, u32[]{:S(2)}) collective-permute-start(f32[384,128]{1,0:T(8,128)S(1)} %get-tuple-element.43), channel_id=1, source_target_pairs={{0,2},{1,3},{2,0},{3,1},{4,6},{5,7},{6,4},{7,5},{8,10},{9,11},{10,... | collective-permute-start | bytes 589832 | tf_op jit(solution)/shard_map/ppermute | solution.py:295
  119.6 1.4 %collective-permute-start.15 = (f32[384,128]{1,0:T(8,128)S(1)}, f32[384,128]{1,0:T(8,128)S(1)}, u32[]{:S(2)}, u32[]{:S(2)}) collective-permute-start(f32[384,128]{1,0:T(8,128)S(1)} %get-tuple-element.44), channel_id=1, source_target_pairs={{0,3},{1,2},{2,1},{3,0},{4,7},{5,6},{6,5},{7,4},{8,11},{9,10},{10,... | collective-permute-start | bytes 589832 | tf_op jit(solution)/shard_map/ppermute | solution.py:295
  121.0 4.1 %shard_map.118.start = f32[384,1024]{1,0:T(8,128)S(1)} custom-call(f32[1,1024]{1,0:T(1,128)S(1)} %bitcast.25, f32[384,128]{1,0:T(8,128)S(1)} %copy-done.22, f32[384,128]{1,0:T(8,128)} %collective-permute-done.5.refs_1_, f32[384,128]{1,0:T(8,128)} %collective-permute-done.6.refs_2_, f32[384,128]{1,0:T(8,128)} %collective-permute-done.7.refs_3_, ...), custom_call_target="tpu_custom_call" | custom-call | flops 1207959552 | bytes 6029312 | tf_op jit(solution)/shard_map/pallas_call | solution.py:267
  125.7 3.3 %collective-permute-done.15.refs_3_ = f32[384,128]{1,0:T(8,128)S(1)} collective-permute-done((f32[384,128]{1,0:T(8,128)S(1)}, f32[384,128]{1,0:T(8,128)S(1)}, u32[]{:S(2)}, u32[]{:S(2)}) %collective-permute-start.15) | collective-permute-done | bytes 196640 | tf_op jit(solution)/shard_map/ppermute | solution.py:295
  129.0 4.7 %shard_map.122 = f32[384,1024]{1,0:T(8,128)} custom-call(f32[384,1024]{1,0:T(8,128)S(1)} %shard_map.118.start, f32[384,128]{1,0:T(8,128)S(1)} %get-tuple-element.41.refs_0_, f32[384,128]{1,0:T(8,128)S(1)} %collective-permute-done.13.refs_1_, f32[384,128]{1,0:T(8,128)S(1)} %collective-permute-done.14.refs_2_, f32[384,128]{1,0:T(8,128)S(1)} %collective-permute-done.15.refs_3_, ...), custom_call_target="tpu_custom_call" | custom-call | flops 1207959552 | bytes 6029312 | tf_op jit(solution)/shard_map/pallas_call | solution.py:267
  (88 shorter events, 13.0 us)
Async XLA Ops:
  0.0 5.4 %collective-permute-start = (f32[1536,256]{1,0:T(8,128)}, f32[1536,256]{1,0:T(8,128)}, u32[]{:S(2)}, u32[]{:S(2)}) collective-permute-start(f32[1536,256]{1,0:T(8,128)} %refs_0_.3), channel_id=1, source_target_pairs={{0,1},{1,0},{2,3},{3,2},{4,5},{5,4},{6,7},{7,6},{8,9},{9,8},{10,11... | collective-permute-start | bytes 4718600 | tf_op jit(solution)/shard_map/ppermute | solution.py:295
  0.5 4.9 %collective-permute-start.1 = (f32[256,1024]{1,0:T(8,128)}, f32[256,1024]{1,0:T(8,128)S(1)}, u32[]{:S(2)}, u32[]{:S(2)}) collective-permute-start(f32[256,1024]{1,0:T(8,128)} %refs_2_.7), channel_id=1, source_target_pairs={{0,1},{1,0},{2,3},{3,2},{4,5},{5,4},{6,7},{7,6},{8,9},{9,8},{10,11... | collective-permute-start | bytes 3145736 | tf_op jit(solution)/shard_map/ppermute | solution.py:295
  11.6 33.4 %copy-start.27 = (s32[1,6]{1,0:T(1,128)S(1)}, s32[1,6]{1,0:T(1,128)}, u32[]{:S(2)}) copy-start(s32[1,6]{1,0:T(1,128)} %param.16) | copy-start | bytes 76
  11.6 33.4 %all-to-all-start = ((f32[8,128,256]{2,1,0:T(8,128)}), f32[8,128,256]{2,1,0:T(8,128)}, u32[]{:S(2)}, u32[]{:S(2)}) async-start(f32[8,128,256]{2,1,0:T(8,128)} %copy-done.12), calls=%async_computation | async-start | bytes 2097152 | tf_op jit(solution)/shard_map/all_to_all | solution.py:298
  19.0 41.1 %collective-permute-start.2 = (f32[1536,256]{1,0:T(8,128)}, f32[1536,256]{1,0:T(8,128)}, u32[]{:S(2)}, u32[]{:S(2)}) collective-permute-start(f32[1536,256]{1,0:T(8,128)} %copy-done.15), channel_id=1, source_target_pairs={{0,2},{1,3},{2,0},{3,1},{4,6},{5,7},{6,4},{7,5},{8,10},{9,11},{10,... | collective-permute-start | bytes 4718600 | tf_op jit(solution)/shard_map/ppermute | solution.py:295
  46.7 1.8 %collective-permute-start.3 = (f32[384,256]{1,0:T(8,128)S(1)}, f32[384,256]{1,0:T(8,128)S(1)}, u32[]{:S(2)}, u32[]{:S(2)}) collective-permute-start(f32[384,256]{1,0:T(8,128)S(1)} %shard_map.113.refs_0_), channel_id=1, source_target_pairs={{0,1},{1,0},{2,3},{3,2},{4,5},{5,4},{6,7},{7,6},{8,9},{9,8},{10,11... | collective-permute-start | bytes 1179656 | tf_op jit(solution)/shard_map/ppermute | solution.py:295
  51.6 12.8 %collective-permute-start.4 = (f32[384,128]{1,0:T(8,128)}, f32[384,128]{1,0:T(8,128)S(1)}, u32[]{:S(2)}, u32[]{:S(2)}) collective-permute-start(f32[384,128]{1,0:T(8,128)} %get-tuple-element.28), channel_id=1, source_target_pairs={{0,2},{1,3},{2,0},{3,1},{4,6},{5,7},{6,4},{7,5},{8,10},{9,11},{10,... | collective-permute-start | bytes 589832 | tf_op jit(solution)/shard_map/ppermute | solution.py:295
  53.1 21.6 %collective-permute-start.9 = (f32[384,128]{1,0:T(8,128)}, f32[384,128]{1,0:T(8,128)}, u32[]{:S(2)}, u32[]{:S(2)}) collective-permute-start(f32[384,128]{1,0:T(8,128)} %copy-done.29), channel_id=1, source_target_pairs={{0,2},{1,3},{2,0},{3,1},{4,6},{5,7},{6,4},{7,5},{8,10},{9,11},{10,... | collective-permute-start | bytes 589832 | tf_op jit(solution)/shard_map/ppermute | solution.py:295
  55.0 5.1 %copy-start.6 = (f32[1536,128]{1,0:T(8,128)S(1)}, f32[1536,128]{1,0:T(8,128)}, u32[]{:S(2)}) copy-start(f32[1536,128]{1,0:T(8,128)} %diag.7) | copy-start | bytes 2359300
  64.4 3.3 %copy-start.23 = (f32[384,128]{1,0:T(8,128)}, f32[384,128]{1,0:T(8,128)S(1)}, u32[]{:S(2)}) copy-start(f32[384,128]{1,0:T(8,128)S(1)} %get-tuple-element.38.refs_0_) | copy-start | bytes 589828
  64.4 25.5 %copy-start.7 = (f32[1536,128]{1,0:T(8,128)S(1)}, f32[1536,128]{1,0:T(8,128)}, u32[]{:S(2)}) copy-start(f32[1536,128]{1,0:T(8,128)} %diag.7) | copy-start | bytes 2359300
  69.3 20.6 %copy-start.5 = (f32[1536,256]{1,0:T(8,128)S(1)}, f32[1536,256]{1,0:T(8,128)}, u32[]{:S(2)}) copy-start(f32[1536,256]{1,0:T(8,128)} %copy-done.4) | copy-start | bytes 4718596
  69.3 27.5 %all-to-all-start.1 = ((f32[8,128,128]{2,1,0:T(8,128)}), f32[8,128,128]{2,1,0:T(8,128)}, u32[]{:S(2)}, u32[]{:S(2)}) async-start(f32[8,128,128]{2,1,0:T(8,128)} %copy-done.20), calls=%async_computation.1 | async-start | bytes 1048576 | tf_op jit(solution)/shard_map/all_to_all | solution.py:298
  74.7 17.9 %copy-start.10 = (f32[1,6,128,128]{3,2,1,0:T(8,128)S(1)}, f32[1,6,128,128]{3,2,1,0:T(8,128)}, u32[]{:S(2)}) copy-start(f32[1,6,128,128]{3,2,1,0:T(8,128)} %param.14) | copy-start | bytes 1179652
  74.7 17.9 %copy-start.24 = (f32[384,128]{1,0:T(8,128)S(1)}, f32[384,128]{1,0:T(8,128)}, u32[]{:S(2)}) copy-start(f32[384,128]{1,0:T(8,128)} %copy-done.23) | copy-start | bytes 589828
  74.7 13.6 %collective-permute-start.10 = (f32[128,1024]{1,0:T(8,128)S(1)}, f32[128,1024]{1,0:T(8,128)}, u32[]{:S(2)}, u32[]{:S(2)}) collective-permute-start(f32[128,1024]{1,0:T(8,128)S(1)} %constant_dynamic-slice_fusion), channel_id=1, source_target_pairs={{0,2},{1,3},{2,0},{3,1},{4,6},{5,7},{6,4},{7,5},{8,10},{9,11},{10,... | collective-permute-start | bytes 1572872 | tf_op jit(solution)/shard_map/ppermute | solution.py:295
  76.3 33.4 %collective-permute-start.8 = (f32[256,1024]{1,0:T(8,128)}, f32[256,1024]{1,0:T(8,128)}, u32[]{:S(2)}, u32[]{:S(2)}) collective-permute-start(f32[256,1024]{1,0:T(8,128)} %refs_4_.3), channel_id=1, source_target_pairs={{0,1},{1,0},{2,3},{3,2},{4,5},{5,4},{6,7},{7,6},{8,9},{9,8},{10,11... | collective-permute-start | bytes 3145736 | tf_op jit(solution)/shard_map/ppermute | solution.py:295
  88.3 13.2 %collective-permute-start.11 = (f32[128,1024]{1,0:T(8,128)}, f32[128,1024]{1,0:T(8,128)}, u32[]{:S(2)}, u32[]{:S(2)}) collective-permute-start(f32[128,1024]{1,0:T(8,128)} %collective-permute-done.10), channel_id=1, source_target_pairs={{0,4},{4,0},{8,12},{12,8},{16,20},{20,16},{24,28},{28,24},{1,5},{5... | collective-permute-start | bytes 1572872 | tf_op jit(solution)/shard_map/ppermute | solution.py:356
  96.8 7.5 %copy-start.11 = (f32[1,6,128,128]{3,2,1,0:T(8,128)S(1)}, f32[1,6,128,128]{3,2,1,0:T(8,128)}, u32[]{:S(2)}) copy-start(f32[1,6,128,128]{3,2,1,0:T(8,128)} %param.14) | copy-start | bytes 1179652
  96.8 7.5 %copy-start.17 = (f32[1536,128]{1,0:T(8,128)S(1)}, f32[1536,128]{1,0:T(8,128)}, u32[]{:S(2)}) copy-start(f32[1536,128]{1,0:T(8,128)} %copy-done.16) | copy-start | bytes 2359300
  96.8 17.5 %all-to-all-start.2 = ((f32[8,128,128]{2,1,0:T(8,128)}), f32[8,128,128]{2,1,0:T(8,128)S(1)}, u32[]{:S(2)}, u32[]{:S(2)}) async-start(f32[8,128,128]{2,1,0:T(8,128)} %get-tuple-element.40), calls=%async_computation.2 | async-start | bytes 1048576 | tf_op jit(solution)/shard_map/all_to_all | solution.py:298
  103.8 17.1 %collective-permute-start.12 = (f32[128,1024]{1,0:T(8,128)}, f32[128,1024]{1,0:T(8,128)}, u32[]{:S(2)}, u32[]{:S(2)}) collective-permute-start(f32[128,1024]{1,0:T(8,128)} %get-tuple-element.46.refs_6_), channel_id=1, source_target_pairs={{0,1},{1,0},{2,3},{3,2},{4,5},{5,4},{6,7},{7,6},{8,9},{9,8},{10,11... | collective-permute-start | bytes 1572872 | tf_op jit(solution)/shard_map/ppermute | solution.py:295
  103.8 25.2 %collective-permute-start.16 = (f32[128,1024]{1,0:T(8,128)}, f32[128,1024]{1,0:T(8,128)S(1)}, u32[]{:S(2)}, u32[]{:S(2)}) collective-permute-start(f32[128,1024]{1,0:T(8,128)} %get-tuple-element.45.refs_6_), channel_id=1, source_target_pairs={{0,1},{1,0},{2,3},{3,2},{4,5},{5,4},{6,7},{7,6},{8,9},{9,8},{10,11... | collective-permute-start | bytes 1572872 | tf_op jit(solution)/shard_map/ppermute | solution.py:295
  104.4 16.6 %copy-start.28 = (f32[1024]{0:T(1024)S(1)}, f32[1024]{0:T(1024)}, u32[]{:S(2)}) copy-start(f32[1024]{0:T(1024)} %param.21) | copy-start | bytes 12292
  108.2 12.8 %copy-start.8 = (f32[256,1024]{1,0:T(8,128)S(1)}, f32[256,1024]{1,0:T(8,128)}, u32[]{:S(2)}) copy-start(f32[256,1024]{1,0:T(8,128)} %refs_4_.3) | copy-start | bytes 3145732
  108.2 9.7 %collective-permute-start.5 = (f32[384,128]{1,0:T(8,128)}, f32[384,128]{1,0:T(8,128)}, u32[]{:S(2)}, u32[]{:S(2)}) collective-permute-start(f32[384,128]{1,0:T(8,128)} %get-tuple-element.32), channel_id=1, source_target_pairs={{0,1},{1,0},{2,3},{3,2},{4,5},{5,4},{6,7},{7,6},{8,9},{9,8},{10,11... | collective-permute-start | bytes 589832 | tf_op jit(solution)/shard_map/ppermute | solution.py:295
  108.2 9.7 %collective-permute-start.6 = (f32[384,128]{1,0:T(8,128)}, f32[384,128]{1,0:T(8,128)}, u32[]{:S(2)}, u32[]{:S(2)}) collective-permute-start(f32[384,128]{1,0:T(8,128)} %get-tuple-element.33), channel_id=1, source_target_pairs={{0,2},{1,3},{2,0},{3,1},{4,6},{5,7},{6,4},{7,5},{8,10},{9,11},{10,... | collective-permute-start | bytes 589832 | tf_op jit(solution)/shard_map/ppermute | solution.py:295
  109.7 9.9 %collective-permute-start.7 = (f32[384,128]{1,0:T(8,128)}, f32[384,128]{1,0:T(8,128)}, u32[]{:S(2)}, u32[]{:S(2)}) collective-permute-start(f32[384,128]{1,0:T(8,128)} %get-tuple-element.34), channel_id=1, source_target_pairs={{0,3},{1,2},{2,1},{3,0},{4,7},{5,6},{6,5},{7,4},{8,11},{9,10},{10,... | collective-permute-start | bytes 589832 | tf_op jit(solution)/shard_map/ppermute | solution.py:295
  115.5 5.5 %copy-start.22 = (f32[384,128]{1,0:T(8,128)S(1)}, f32[384,128]{1,0:T(8,128)}, u32[]{:S(2)}) copy-start(f32[384,128]{1,0:T(8,128)} %copy-done.21) | copy-start | bytes 589828
  117.9 7.3 %collective-permute-start.13 = (f32[384,128]{1,0:T(8,128)S(1)}, f32[384,128]{1,0:T(8,128)S(1)}, u32[]{:S(2)}, u32[]{:S(2)}) collective-permute-start(f32[384,128]{1,0:T(8,128)S(1)} %get-tuple-element.42), channel_id=1, source_target_pairs={{0,1},{1,0},{2,3},{3,2},{4,5},{5,4},{6,7},{7,6},{8,9},{9,8},{10,11... | collective-permute-start | bytes 589832 | tf_op jit(solution)/shard_map/ppermute | solution.py:295
  118.0 7.8 %collective-permute-start.14 = (f32[384,128]{1,0:T(8,128)S(1)}, f32[384,128]{1,0:T(8,128)S(1)}, u32[]{:S(2)}, u32[]{:S(2)}) collective-permute-start(f32[384,128]{1,0:T(8,128)S(1)} %get-tuple-element.43), channel_id=1, source_target_pairs={{0,2},{1,3},{2,0},{3,1},{4,6},{5,7},{6,4},{7,5},{8,10},{9,11},{10,... | collective-permute-start | bytes 589832 | tf_op jit(solution)/shard_map/ppermute | solution.py:295
  119.6 9.4 %collective-permute-start.15 = (f32[384,128]{1,0:T(8,128)S(1)}, f32[384,128]{1,0:T(8,128)S(1)}, u32[]{:S(2)}, u32[]{:S(2)}) collective-permute-start(f32[384,128]{1,0:T(8,128)S(1)} %get-tuple-element.44), channel_id=1, source_target_pairs={{0,3},{1,2},{2,1},{3,0},{4,7},{5,6},{6,5},{7,4},{8,11},{9,10},{10,... | collective-permute-start | bytes 589832 | tf_op jit(solution)/shard_map/ppermute | solution.py:295
  (18 other events, 24.1 us)
where the time goes:
time: 135 us; the launch traced here: 134 us
  waiting for transfers between devices  46.5 us (34%)
  Pallas kernels  41.8 us (31%)
  starting transfers between devices  29.1 us (22%)
  local copies, waits for them, and re-layouts  12.1 us (9%)
  other arithmetic  3.73 us (3%)
    all_to_all x3, waiting for transfers between devices, dom_exchange(): return lax.all_to_all(x, 'dom', split_axis=0, concat_axis=0, tiled=True)  28.8 us
    ppermute x16, waiting for transfers between devices, feat_send(): lax.ppermute(x, 'feat', [(f, feat_target(f, dh, dl)) for f in range(feats)])  17.7 us
    all_to_all x3, starting transfers between devices, dom_exchange(): return lax.all_to_all(x, 'dom', split_axis=0, concat_axis=0, tiled=True)  16.4 us
    pallas_call x4, Pallas kernels, partial_sums(): pl.pallas_call(functools.partial(partial_body, count), out_shape=[f32(row...  12.9 us
    ppermute x16, starting transfers between devices, feat_send(): lax.ppermute(x, 'feat', [(f, feat_target(f, dh, dl)) for f in range(feats)])  11.1 us
    unnamed x60, local copies, waits for them, and re-layouts  10.8 us
    pallas_call x2, Pallas kernels, add_product(): pl.pallas_call(functools.partial(product_body, count), out_shape=f32(rows...  8.78 us
    pallas_call x2, Pallas kernels, hidden_blocks(): pl.pallas_call(functools.partial(hidden_body, count, offset), out_shape=[...  6.45 us
  transfers between devices with their start and end apart: 20, of which 7 were waited for; matrix products, arithmetic and copies ran while one was open for 4% of the time, Pallas kernels for 24%

commit v1 on v0

v1 whole, which is shorter than its diff:
```python
import functools

import jax
import jax.numpy as jnp
from jax import lax
from jax.experimental import pallas as pl
from jax.experimental.pallas import tpu as pltpu
from jax.sharding import PartitionSpec as P

LANES = 128
TOUCH = 2
VMEM_LIMIT = 24 * 1024 * 1024
VMEM = pl.BlockSpec(memory_space=pltpu.VMEM)
SMEM = pl.BlockSpec(memory_space=pltpu.SMEM)
HBM = pl.BlockSpec(memory_space=pltpu.HBM)
PARAMS = pltpu.CompilerParams(vmem_limit_bytes=VMEM_LIMIT)


def dot3(a, b):
    return jnp.dot(a, b, precision=lax.Precision.HIGH, preferred_element_type=jnp.float32)


def two_parts(x):
    high = x.astype(jnp.bfloat16)
    return high, (x - high.astype(jnp.float32)).astype(jnp.bfloat16)


def left_parts(x):
    high, low = two_parts(x)
    return jnp.concatenate([high, low, high], axis=1)


def right_parts(w):
    high, low = two_parts(w)
    return jnp.concatenate([high, high, low], axis=0)


def f32(*dims):
    return jax.ShapeDtypeStruct(dims, jnp.float32)


def rows_at(index, height):
    return pl.ds(pl.multiple_of(index * height, height), height)


def scratch(*dims):
    return pltpu.VMEM(dims, jnp.float32)


def start_all(pairs, sems, first):
    copies = [pltpu.make_async_copy(a, b, sems.at[first + i]) for i, (a, b) in enumerate(pairs)]
    for copy in copies:
        copy.start()
    return copies


def wait_all(copies):
    for copy in copies:
        copy.wait()


def cost(flops):
    return pl.CostEstimate(flops=flops, bytes_accessed=0, transcendentals=0)


def slice_body(index_ref, source, out, sem):
    wait_all(start_all([(source.at[rows_at(index_ref[0], out.shape[0])], out)], sem, 0))


def row_block(index, source, height):
    return pl.pallas_call(
        slice_body,
        out_shape=f32(height, source.shape[1]),
        in_specs=[SMEM, HBM],
        out_specs=HBM,
        scratch_shapes=[pltpu.SemaphoreType.DMA((1,))],
        compiler_params=PARAMS,
    )(index, source)


def outgoing_body(want_ref, features, spread, blocks, held, spread_in, sems):
    count, tile, cols = held.shape
    chunk = spread_in.shape[2]
    last = features.shape[0] // tile - 1
    rows = [rows_at(jnp.minimum(want_ref[d], last), tile) for d in range(count)]
    loads = start_all([(features.at[r], held.at[d]) for d, r in enumerate(rows)], sems, 0)
    loads += start_all([(spread.at[r], spread_in.at[d]) for d, r in enumerate(rows)], sems, count)
    stores = []
    for d in range(count):
        loads[d].wait()
        loads[count + d].wait()
        for c in range(cols // chunk):
            lanes = pl.ds(c * chunk, chunk)
            held[d, :, lanes] = held[d, :, lanes] * spread_in[d]
        stores += start_all([(held.at[d], blocks.at[d])], sems, 2 * count + d)
    wait_all(stores)


def outgoing_blocks(want, features, spread, tile):
    cols, chunk = features.shape[1], spread.shape[1]
    count = want.shape[0]
    return pl.pallas_call(
        outgoing_body,
        out_shape=f32(count, tile, cols),
        in_specs=[SMEM, HBM, HBM],
        out_specs=HBM,
        scratch_shapes=[
            scratch(count, tile, cols),
            scratch(count, tile, chunk),
            pltpu.SemaphoreType.DMA((3 * count,)),
        ],
        compiler_params=PARAMS,
    )(want, features, spread)


def partial_body(count, at, steps, carried, place_ref, *refs):
    lefts, rights, refs = refs[:count], refs[count : 2 * count], refs[2 * count :]
    passing, refs = refs[: len(carried)], refs[len(carried) :]
    outs, (left, right, result, sems) = refs[:-4], refs[-4:]
    cols = lefts[0].shape[1]
    chunk = outs[0].shape[1]
    lanes = pl.ds(pl.multiple_of(place_ref[at] * cols, cols), cols)
    used = 0
    weights_in = start_all([(w.at[:, lanes], right.at[j]) for j, w in enumerate(rights)], sems, used)
    used += count
    stores = start_all(
        [(p, outs[o].at[pl.ds(offset, p.shape[0])]) for p, (o, offset) in zip(passing, carried)], sems, used
    )
    used += len(carried)
    loads = []
    for start, stop, _ in steps:
        rows = pl.ds(start, stop - start)
        pairs = [(x.at[rows], left.at[rows, pl.ds(j * cols, cols)]) for j, x in enumerate(lefts)]
        loads.append(start_all(pairs, sems, used))
        used += count
    wait_all(weights_in)
    weight = right_parts(jnp.concatenate([right[j] for j in range(count)], axis=0))
    for (start, stop, targets), ready in zip(steps, loads):
        wait_all(ready)
        rows = pl.ds(start, stop - start)
        result[rows, :] = jnp.dot(left_parts(left[rows, :]), weight, preferred_element_type=jnp.float32)
        pairs = [
            (result.at[rows, pl.ds(c * chunk, chunk)], outs[o].at[pl.ds(offset, stop - start)])
            for c, o, offset in targets
        ]
        stores += start_all(pairs, sems, used)
        used += len(pairs)
    wait_all(stores)


def partial_sums(place, at, lefts, weights, steps, shapes, passing=(), carried=()):
    rows, cols = lefts[0].shape
    depth = weights[0].shape[0]
    count = len(lefts)
    copies = count + len(carried) + sum(count + len(targets) for _, _, targets in steps)
    return pl.pallas_call(
        functools.partial(partial_body, count, at, steps, carried),
        out_shape=[f32(*s) for s in shapes],
        in_specs=[SMEM] + [HBM] * (2 * count + len(passing)),
        out_specs=[HBM] * len(shapes),
        scratch_shapes=[
            scratch(rows, count * cols),
            scratch(count, depth, cols),
            scratch(rows, cols),
            pltpu.SemaphoreType.DMA((copies,)),
        ],
        compiler_params=PARAMS,
        cost_estimate=cost(6 * rows * depth * cols * count),
    )(place, *lefts, *weights, *passing)


def chosen_body(source_ref, incoming, chosen, sems):
    tile = incoming.shape[1]
    groups = chosen.shape[0] // tile
    pairs = [(incoming.at[source_ref[TOUCH * g]], chosen.at[pl.ds(g * tile, tile)]) for g in range(groups)]
    wait_all(start_all(pairs, sems, 0))


def chosen_blocks(source, incoming):
    tile, cols = incoming.shape[1:]
    groups = source.shape[0] // TOUCH
    return pl.pallas_call(
        chosen_body,
        out_shape=f32(groups * tile, cols),
        in_specs=[SMEM, HBM],
        out_specs=HBM,
        scratch_shapes=[pltpu.SemaphoreType.DMA((groups,))],
        compiler_params=PARAMS,
    )(source, incoming)


def received_pairs(layout, received, recv_in):
    return [
        (received[r].at[pl.ds(start, stop - start)], recv_in.at[h, pl.ds(offset, stop - start)])
        for h, r, start, stop, offset in layout
    ]


def own_total(diag_in, spread_in, own_in, recv_in, total):
    tile = diag_in.shape[1]
    for i in range(diag_in.shape[0] // tile):
        rows = pl.ds(i * tile, tile)
        mixed = own_in[rows, :]
        for h in range(recv_in.shape[0]):
            mixed = mixed + recv_in[h, rows, :]
        total[rows, :] = dot3(diag_in[rows, :], mixed * spread_in[rows, :])


def own_body(layout, diag, spread, own, *refs):
    received, (base, diag_in, spread_in, own_in, recv_in, total, sems) = refs[:-7], refs[-7:]
    pairs = [(diag, diag_in), (spread, spread_in), (own, own_in)]
    wait_all(start_all(pairs + received_pairs(layout, received, recv_in), sems, 0))
    own_total(diag_in, spread_in, own_in, recv_in, total)
    wait_all(start_all([(total, base)], sems, 3 + len(layout)))


def own_part(diag, spread, own, received, layout, others):
    return pl.pallas_call(
        functools.partial(own_body, layout),
        out_shape=f32(*own.shape),
        in_specs=[HBM] * (3 + len(received)),
        out_specs=HBM,
        scratch_shapes=[scratch(*a.shape) for a in (diag, spread, own)]
        + [scratch(others, *own.shape), scratch(*own.shape), pltpu.SemaphoreType.DMA((4 + len(layout),))],
        compiler_params=PARAMS,
        cost_estimate=cost(0),
    )(diag, spread, own, *received)


def hidden_body(
    count, reach, layout, lane_offset, row_ref, want_ref, first_ref, bias, base, remote, spread, diag, *refs
):
    remote_sums, refs = refs[:count], refs[count:]
    received, refs = refs[:reach], refs[reach:]
    blocks, base_out, total, remote_in, spread_in, diag_in, scaled, sums_in, recv_in, sems = refs
    tiles, tile = remote.shape[:2]
    parts = blocks.shape[0]
    chunk = total.shape[1]
    height = sums_in.shape[1]
    begin = total if reach == 0 else scaled
    pairs = [(base, begin), (spread, spread_in), (diag, diag_in)]
    pairs += received_pairs(layout, received, recv_in)
    late = [(remote, remote_in)]
    late += [(s.at[pl.ds(s.shape[0] - height, height)], sums_in.at[j]) for j, s in enumerate(remote_sums)]
    if reach == 0:
        tail = start_all(late, sems, 0)
        first = start_all(pairs, sems, len(late))
        wait_all(first[:1])
    else:
        first = start_all(pairs, sems, 0)
        tail = start_all(late, sems, len(pairs))
        wait_all(first)
        own_total(diag_in, spread_in, scaled, recv_in, total)
    wait_all(tail)
    for g in range(tiles // TOUCH):
        rows = pl.ds(g * tile, tile)
        block = sums_in[0, rows, :]
        for j in range(1, count):
            block = block + sums_in[j, rows, :]
        for k in range(TOUCH * g, TOUCH * g + TOUCH):
            total[rows_at(row_ref[k], tile), :] += dot3(remote_in[k], block)
    lanes = pl.ds(pl.multiple_of(first_ref[0] + lane_offset, chunk), chunk)
    shift = bias[:, lanes]
    if reach == 0:
        wait_all(first[1:])
    scaled[...] = jnp.maximum(total[...] * spread_in[...] + shift, 0.0) * spread_in[...]
    used = len(pairs) + len(late)
    last = scaled.shape[0] // tile - 1
    copies = start_all(
        [(scaled.at[rows_at(jnp.minimum(want_ref[d], last), tile)], blocks.at[d]) for d in range(parts)],
        sems,
        used,
    )
    for i in range(last + 1):
        rows = pl.ds(i * tile, tile)
        total[rows, :] = dot3(diag_in[rows, :], scaled[rows, :])
    copies += start_all([(total, base_out)], sems, used + parts)
    wait_all(copies)


def hidden_blocks(
    row, want, first, lane_offset, bias, base, remote, spread, diag, remote_sums, received, layout, others, flops
):
    rows, chunk = base.shape
    tile = diag.shape[1]
    parts = want.shape[0]
    count = len(remote_sums)
    height = remote.shape[0] // TOUCH * tile
    return pl.pallas_call(
        functools.partial(hidden_body, count, len(received), layout, lane_offset),
        out_shape=[f32(parts, tile, chunk), f32(rows, chunk)],
        in_specs=[SMEM] * 3 + [VMEM] + [HBM] * (4 + count + len(received)),
        out_specs=[HBM, HBM],
        scratch_shapes=[scratch(*a.shape) for a in (base, remote, spread, diag, base)]
        + [scratch(count, height, chunk), scratch(others, *base.shape)]
        + [pltpu.SemaphoreType.DMA((5 + len(layout) + count + parts,))],
        compiler_params=PARAMS,
        cost_estimate=cost(flops),
    )(row, want, first, bias, base, remote, spread, diag, *remote_sums, *received)


def pieces_body(source_ref, row_ref, place_ref, base, remote, spread, incoming, *refs):
    pieces, (total, remote_in, spread_in, incoming_in, sems) = refs[:-5], refs[-5:]
    tiles, tile = remote.shape[:2]
    early = start_all(
        [(incoming, incoming_in), (remote, remote_in), (base, total), (spread, spread_in)], sems, 0
    )
    wait_all(early[:3])
    for k in range(tiles):
        total[rows_at(row_ref[k], tile), :] += dot3(remote_in[k], incoming_in[source_ref[k]])
    wait_all(early[3:])
    total[...] = total[...] * spread_in[...]
    height = pieces[0].shape[0]
    pairs = [(total.at[rows_at(place_ref[j], height)], p) for j, p in enumerate(pieces)]
    wait_all(start_all(pairs, sems, 4))


def feature_pieces(source, row, place, base, remote, spread, incoming):
    rows, chunk = base.shape
    feats = place.shape[0]
    return pl.pallas_call(
        pieces_body,
        out_shape=[f32(rows // feats, chunk)] * feats,
        in_specs=[SMEM] * 3 + [HBM] * 4,
        out_specs=[HBM] * feats,
        scratch_shapes=[scratch(*a.shape) for a in (base, remote, spread, incoming)]
        + [pltpu.SemaphoreType.DMA((4 + feats,))],
        compiler_params=PARAMS,
        cost_estimate=cost(0),
    )(source, row, place, base, remote, spread, incoming)


def product_body(count, choices, turn_ref, start, *refs):
    pieces, weights, (out, left) = refs[:count], refs[count:-2], refs[-2:]
    chunk = pieces[0].shape[1]

    @pl.when(pl.program_id(0) == 0)
    def _():
        left[...] = left_parts(jnp.concatenate([p[...] for p in pieces], axis=1))

    blocks, at = [], 0
    for number in choices:
        block = weights[at][...]
        for k in range(1, number):
            block = jnp.where(turn_ref[0] == k, weights[at + k][...], block)
        blocks.append(block)
        at += number
    right = right_parts(jnp.concatenate(blocks, axis=0))
    out[...] = start[...] + jnp.dot(left[...], right, preferred_element_type=jnp.float32)


def add_product(turn, start, pieces, weights):
    rows, chunk = pieces[0].shape
    width = start.shape[1]
    step = min(2 * LANES, width)
    count = len(pieces)
    flat = [w for group in weights for w in group]
    return pl.pallas_call(
        functools.partial(product_body, count, [len(group) for group in weights]),
        out_shape=f32(rows, width),
        grid_spec=pltpu.PrefetchScalarGridSpec(
            num_scalar_prefetch=1,
            grid=(width // step,),
            in_specs=[pl.BlockSpec((start.shape[0], step), lambda j, turn: (0, j))]
            + [pl.BlockSpec((rows, chunk), lambda j, turn: (0, 0))] * count
            + [pl.BlockSpec((chunk, step), lambda j, turn, c=c: (c, j)) for _, c in flat],
            out_specs=pl.BlockSpec((rows, step), lambda j, turn: (0, j)),
            scratch_shapes=[pltpu.VMEM((rows, 3 * count * chunk), jnp.bfloat16)],
        ),
        compiler_params=PARAMS,
        cost_estimate=cost(6 * count * rows * chunk * width),
    )(turn, start, *pieces, *[w for w, _ in flat])


def solution(mesh):
    parts = mesh.shape["dom"]
    feats = mesh.shape["feat"]
    sides = 2 if feats % 2 == 0 else 1
    halves = feats // sides
    others = list(range(1, halves))

    def feat_target(f, dh, dl):
        return (f // sides + dh) % halves * sides + (f % sides + dl) % sides

    def feat_send(x, dh, dl):
        return lax.ppermute(x, "feat", [(f, feat_target(f, dh, dl)) for f in range(feats)])

    def dom_exchange(x):
        return lax.all_to_all(x, "dom", split_axis=0, concat_axis=0, tiled=True)

    def per_device(
        features,
        degree,
        diag_adj,
        remote_adj,
        read_block,
        tile_src,
        tile_row,
        w_first,
        b_first,
        w_second,
        b_second,
    ):
        part, cols = features.shape
        tile = diag_adj.shape[1]
        blocks = part // tile
        remote = remote_adj[0]
        chunk = LANES if cols % LANES == 0 else cols
        chunks = cols // chunk
        f = lax.axis_index("feat")
        want, source, row = read_block[0], tile_src[0], tile_row[0]
        shifts = [(dh, dl) for dh in range(halves) for dl in range(sides)]
        place = jnp.stack([jnp.asarray(feat_target(f, dh, dl), jnp.int32) for dh, dl in shifts])
        first = jnp.reshape(jnp.asarray(f * cols, jnp.int32), (1,))
        bias = b_first[None, :]

        x_all = [features] + [feat_send(features, 0, dl) for dl in range(1, sides)]
        w_all = [w_first] + [feat_send(w_first, 0, dl) for dl in range(1, sides)]

        shares = chunks if parts % chunks == 0 else 1
        share = jnp.reshape(jnp.asarray(lax.axis_index("dom") % shares, jnp.int32), (1,))
        share_rows = w_second.shape[0] // shares

        def share_send(x, k):
            pairs = [(s, s // shares * shares + (s % shares + k) % shares) for s in range(parts)]
            return lax.ppermute(x, "dom", pairs)

        w2_sent = row_block(share, w_second, share_rows)
        w2_got = [feat_send(w2_sent, dh, 0) for dh in others]

        scaling = lax.rsqrt(degree.astype(jnp.float32))
        spread = jnp.broadcast_to(scaling[:, None], (part, chunk))
        outgoing = outgoing_blocks(want, features, spread, tile)
        incoming = dom_exchange(outgoing)

        early = blocks * 5 // 12 * tile if chunks > 1 else part
        late = part - early
        marks = sorted({0, early // 2 // tile * tile, early, early + late // 2 // tile * tile, part})
        spans = list(zip(marks[:-1], marks[1:]))
        x_all[0], _ = lax.optimization_barrier((features, outgoing))
        send_steps = []
        for start, stop in spans:
            targets = [(0, 0, start)]
            for c in range(1, chunks):
                if stop <= early:
                    targets.append((c, 0, part + (c - 1) * early + start))
                else:
                    targets.append((c, 1, (c - 1) * late + start - early))
            send_steps.append((start, stop, targets))
        send_shapes = [(part + (chunks - 1) * early, chunk)]
        if late > 0:
            send_shapes.append(((chunks - 1) * late, chunk))
        sends = [partial_sums(place, dh * sides, x_all, w_all, send_steps, send_shapes) for dh in others]
        front = [feat_send(x[0], dh, 0) for dh, x in zip(others, sends)]

        own_steps = [(a, b, [(c, c, a) for c in range(chunks)]) for a, b in spans]
        own = partial_sums(place, 0, x_all, w_all, own_steps, [(part, chunk)] * chunks)

        w2_got, _ = lax.optimization_barrier((w2_got, [x[0] for x in sends]))
        w2_groups = [[got] + [share_send(got, k) for k in range(1, shares)] for got in w2_got]
        w2_core = [w_second] + [feat_send(w_second, 0, dl) for dl in range(1, sides)]
        w2_far = [[feat_send(w, 0, dl) if dl > 0 else w for w in g] for g in w2_groups for dl in range(sides)]

        incoming, own, w2_core, w2_far = lax.optimization_barrier((incoming, own, w2_core, w2_far))
        chosen = chosen_blocks(source, incoming)
        chosen_all = [chosen] + [feat_send(chosen, 0, dl) for dl in range(1, sides)]
        height = chosen.shape[0]
        tail_rows = (chunks - 1) * late
        remote_steps = [
            (0, height, [(0, 0, 0)] + [(c, 1, tail_rows + (c - 1) * height) for c in range(1, chunks)])
        ]
        remote_shapes = [(height, chunk)]
        if chunks > 1:
            remote_shapes.append((tail_rows + (chunks - 1) * height, chunk))
        remote_sends = [
            partial_sums(place, dh * sides, chosen_all, w_all, remote_steps, remote_shapes, x[1:], [(1, 0)] * len(x[1:]))
            for dh, x in zip(others, sends)
        ]
        remote_front = [feat_send(x[0], dh, 0) for dh, x in zip(others, remote_sends)]
        rest = [feat_send(x[1], dh, 0) for dh, x in zip(others, remote_sends)] if chunks > 1 else []
        own_remote_steps = [(0, height, [(c, c, 0) for c in range(chunks)])]
        remote_own = partial_sums(
            place, 0, chosen_all, w_all, own_remote_steps, [(height, chunk)] * chunks
        )

        reach = len(others)
        first_layout = [(h, h, 0, part, 0) for h in range(reach)]
        base = own_part(diag_adj, spread, own[0], front, first_layout, reach)
        collected = []
        outgoing = None
        for c in range(chunks):
            if c == 0:
                begin, received, layout = base, [], []
                remote_sums = [remote_own[0]] + remote_front
            else:
                begin, _ = lax.optimization_barrier((own[c], outgoing))
                received = front + rest
                layout = []
                for h in range(reach):
                    layout.append((h, h, part + (c - 1) * early, part + c * early, 0))
                    if late > 0:
                        layout.append((h, reach + h, (c - 1) * late, c * late, early))
                ends = tail_rows + c * height
                remote_sums = [remote_own[c]] + [r if ends == r.shape[0] else r[:ends] for r in rest]
            outgoing, base_next = hidden_blocks(
                row,
                want,
                first,
                c * chunk,
                bias,
                begin,
                remote,
                spread,
                diag_adj,
                remote_sums,
                received,
                layout,
                reach,
                0 if c == 0 else 10**11 // 2,
            )
            incoming = dom_exchange(outgoing)
            pieces = feature_pieces(source, row, place, base_next, remote, spread, incoming)
            collected.append(
                [p if dh == 0 and dl == 0 else feat_send(p, dh, dl) for (dh, dl), p in zip(shifts, pieces)]
            )

        out = b_second[None, :]
        for c in range(chunks):
            weights = [[(w, c)] for w in w2_core]
            if shares == 1:
                weights += [[(group[0], c)] for group in w2_far]
            else:
                weights += [[(w, 0) for w in group] for group in w2_far]
            out = add_product((share - c) % shares, out, collected[c], weights)
        return out

    return jax.shard_map(
        per_device,
        mesh=mesh,
        in_specs=(
            P("dom", "feat"),
            P("dom"),
            P("dom", None),
            P("dom", None, None, None),
            P("dom", None),
            P("dom", None),
            P("dom", None),
            P("feat", None),
            P(),
            P("feat", None),
            P(),
        ),
        out_specs=P(("dom", "feat"), None),
        check_vma=False,
    )
```

time: 135 us -> 169 us (1.25)
  Pallas kernels: 41.8 us -> 60.6 us
  waiting for transfers between devices: 46.5 us -> 59.6 us
  local copies, waits for them, and re-layouts: 12.1 us -> 17.6 us
  other arithmetic: 3.73 us -> 0.78 us
    pallas_call x11, Pallas kernels: 34.7 us -> 52.7 us  [the longest x1 17 us: row_block(): pl.pallas_call(slice_body, out_shape=f32(height, source.shape[1]), in_spe...]
    ppermute x16, waiting for transfers between devices: 17.7 us -> 34.4 us  [feat_send(): lax.ppermute(x, 'feat', [(f, feat_target(f, dh, dl)) for f in range(feats)])]
    all_to_all x3, waiting for transfers between devices: 28.8 us -> 14.2 us  [dom_exchange(): return lax.all_to_all(x, 'dom', split_axis=0, concat_axis=0, tiled=True)]
    ppermute x1, waiting for transfers between devices: 0.01 us -> 11 us  [share_send(): return lax.ppermute(x, 'dom', pairs)]
    unnamed x60 -> x64, local copies, waits for them, and re-layouts: 10.8 us -> 17.4 us
    select_n x1 -> x0, other arithmetic: 2.29 us -> none  [per_device(): block = lax.select_n((share - c) % shares, *group)]
  transfers between devices with their start and end apart: 20 -> 20, of which waited for: 7 -> 9; matrix products, arithmetic and copies ran while one was open for 4% -> 1% of each run, Pallas kernels for 24% -> 33%
where the time goes in v1:
time: 169 us; the launch traced here: 168 us
  Pallas kernels  60.6 us (36%)
  waiting for transfers between devices  59.6 us (35%)
  starting transfers between devices  28.7 us (17%)
  local copies, waits for them, and re-layouts  17.6 us (10%)
    ppermute x16, waiting for transfers between devices, feat_send(): lax.ppermute(x, 'feat', [(f, feat_target(f, dh, dl)) for f in range(feats)])  34.4 us
    unnamed x64, local copies, waits for them, and re-layouts  17.4 us
    all_to_all x3, starting transfers between devices, dom_exchange(): return lax.all_to_all(x, 'dom', split_axis=0, concat_axis=0, tiled=True)  17.1 us
    pallas_call x1, Pallas kernels, row_block(): pl.pallas_call(slice_body, out_shape=f32(height, source.shape[1]), in_spe...  17 us
    all_to_all x3, waiting for transfers between devices, dom_exchange(): return lax.all_to_all(x, 'dom', split_axis=0, concat_axis=0, tiled=True)  14.2 us
    pallas_call x4, Pallas kernels, partial_sums(): pl.pallas_call(functools.partial(partial_body, count, at, steps, carried)...  13.3 us
    ppermute x1, waiting for transfers between devices, share_send(): return lax.ppermute(x, 'dom', pairs)  11 us
    ppermute x16, starting transfers between devices, feat_send(): lax.ppermute(x, 'feat', [(f, feat_target(f, dh, dl)) for f in range(feats)])  9.87 us
  transfers between devices with their start and end apart: 20, of which 9 were waited for; matrix products, arithmetic and copies ran while one was open for 1% of the time, Pallas kernels for 33%

profile of v1, /device:TPU:0, one launch (start us, length us, event | category | flops | bytes accessed | tf_op | source)
XLA Modules:
  0.0 167.8 jit_solution(9355482672964345196)
XLA Ops:
  1.5 1.4 copy-done.1
  3.6 4.3 %shard_map.109 = f32[8,128,256]{2,1,0:T(8,128)S(1)} custom-call(s32[8]{0:T(128)S(1)} %bitcast.26, f32[1536,256]{1,0:T(8,128)S(1)} %copy-done.1, f32[1536,128]{1,0:T(8,128)S(1)} %broadcast_in_dim.14.spread), custom_call_target="tpu_custom_call" | custom-call | tf_op jit(solution)/shard_map/pallas_call | solution.py:102
  8.8 7.4 %all-to-all-start = ((f32[8,128,256]{2,1,0:T(8,128)}), f32[8,128,256]{2,1,0:T(8,128)}, u32[]{:S(2)}, u32[]{:S(2)}) async-start(f32[8,128,256]{2,1,0:T(8,128)} %copy-done.3), calls=%async_computation | async-start | bytes 2097152 | tf_op jit(solution)/shard_map/all_to_all | solution.py:389
  16.2 17.0 %shard_map.111 = f32[128,1024]{1,0:T(8,128)} custom-call(s32[1]{0:T(128)} %bitcast.index_ref, f32[256,1024]{1,0:T(8,128)} %refs_4_.1), custom_call_target="tpu_custom_call" | custom-call | tf_op jit(solution)/shard_map/pallas_call | solution.py:71
  33.2 1.6 collective-permute-start.3
  34.9 1.4 copy-done.2
  36.3 5.3 %shard_map.112 = (f32[2176,128]{1,0:T(8,128)}, f32[896,128]{1,0:T(8,128)S(1)}) custom-call(s32[4]{0:T(128)S(1)} %pad_add_fusion.place_ref, f32[1536,256]{1,0:T(8,128)S(1)} %copy-done.2, f32[1536,256]{1,0:T(8,128)} %collective-permute-done.refs_1_, f32[256,1024]{1,0:T(8,128)S(1)} %copy-done, f32[256,1024]{1,0:T(8,128)S(1)} %collective-permute-done.1.refs_3_), custom_call_target="tpu_custom_call" | custom-call | flops 1207959552 | tf_op jit(solution)/shard_map/pallas_call | solution.py:156
  42.4 4.6 %collective-permute-done.3.refs_6_ = f32[128,1024]{1,0:T(8,128)S(1)} collective-permute-done((f32[128,1024]{1,0:T(8,128)}, f32[128,1024]{1,0:T(8,128)S(1)}, u32[]{:S(2)}, u32[]{:S(2)}) %collective-permute-start.3) | collective-permute-done | bytes 524320 | tf_op jit(solution)/shard_map/ppermute | solution.py:386
  47.0 1.7 %collective-permute-start.4 = (f32[128,1024]{1,0:T(8,128)S(1)}, f32[128,1024]{1,0:T(8,128)}, u32[]{:S(2)}, u32[]{:S(2)}) collective-permute-start(f32[128,1024]{1,0:T(8,128)S(1)} %collective-permute-done.3.refs_6_), channel_id=1, source_target_pairs={{0,4},{4,0},{8,12},{12,8},{16,20},{20,16},{24,28},{28,24},{1,5},{5... | collective-permute-start | bytes 1572872 | tf_op jit(solution)/shard_map/ppermute | solution.py:426
  48.8 11.0 %collective-permute-done.4.refs_7_ = f32[128,1024]{1,0:T(8,128)} collective-permute-done((f32[128,1024]{1,0:T(8,128)S(1)}, f32[128,1024]{1,0:T(8,128)}, u32[]{:S(2)}, u32[]{:S(2)}) %collective-permute-start.4) | collective-permute-done | bytes 524320 | tf_op jit(solution)/shard_map/ppermute | solution.py:426
  59.8 1.5 collective-permute-start.7
  61.3 4.7 %shard_map.110 = (f32[1536,128]{1,0:T(8,128)S(1)}, f32[1536,128]{1,0:T(8,128)S(1)}) custom-call(s32[4]{0:T(128)S(1)} %pad_add_fusion.place_ref, f32[1536,256]{1,0:T(8,128)S(1)} %copy-done.2, f32[1536,256]{1,0:T(8,128)} %collective-permute-done.refs_1_, f32[256,1024]{1,0:T(8,128)S(1)} %copy-done, f32[256,1024]{1,0:T(8,128)S(1)} %collective-permute-done.1.refs_3_), custom_call_target="tpu_custom_call" | custom-call | flops 1207959552 | tf_op jit(solution)/shard_map/pallas_call | solution.py:156
  67.9 1.6 shard_map.114.refs_0_
  69.8 1.5 collective-permute-done.8.refs_1_
  71.3 2.0 %shard_map.116 = (f32[384,128]{1,0:T(8,128)}, f32[1280,128]{1,0:T(8,128)}) custom-call(s32[4]{0:T(128)S(1)} %pad_add_fusion.place_ref, f32[384,256]{1,0:T(8,128)S(1)} %shard_map.114.refs_0_, f32[384,256]{1,0:T(8,128)S(1)} %collective-permute-done.8.refs_1_, f32[256,1024]{1,0:T(8,128)S(1)} %copy-done, f32[256,1024]{1,0:T(8,128)S(1)} %collective-permute-done.1.refs_3_, ...), custom_call_target="tpu_custom_call" | custom-call | flops 301989888 | tf_op jit(solution)/shard_map/pallas_call | solution.py:156
  73.9 1.5 collective-permute-start.9
  75.5 12.0 %collective-permute-done.7.refs_0_.refs_2_ = f32[2176,128]{1,0:T(8,128)} collective-permute-done((f32[2176,128]{1,0:T(8,128)}, f32[2176,128]{1,0:T(8,128)}, u32[]{:S(2)}, u32[]{:S(2)}) %collective-permute-start.7) | collective-permute-done | bytes 1114144 | tf_op jit(solution)/shard_map/ppermute | solution.py:386
  89.8 1.9 %shard_map.113.base = f32[1536,128]{1,0:T(8,128)S(1)} custom-call(f32[1536,128]{1,0:T(8,128)S(1)} %copy-done.7, f32[1536,128]{1,0:T(8,128)S(1)} %broadcast_in_dim.14.spread, f32[1536,128]{1,0:T(8,128)S(1)} %copy-done.14, f32[2176,128]{1,0:T(8,128)} %collective-permute-done.7.refs_0_.refs_2_), custom_call_target="tpu_custom_call" | custom-call | tf_op jit(solution)/shard_map/pallas_call | solution.py:218
  93.0 12.3 %collective-permute-done.9.refs_1_ = f32[384,128]{1,0:T(8,128)S(1)} collective-permute-done((f32[384,128]{1,0:T(8,128)}, f32[384,128]{1,0:T(8,128)S(1)}, u32[]{:S(2)}, u32[]{:S(2)}) %collective-permute-start.9) | collective-permute-done | bytes 196640 | tf_op jit(solution)/shard_map/ppermute | solution.py:386
  105.3 2.9 %shard_map.117 = (f32[8,128,128]{2,1,0:T(8,128)}, f32[1536,128]{1,0:T(8,128)S(1)}) custom-call(s32[6]{0:T(128)S(1)} %bitcast.19, s32[8]{0:T(128)S(1)} %bitcast.27, s32[1]{0:T(128)} %bitcast.9.first_ref, f32[1,1024]{1,0:T(1,128)S(1)} %bitcast.23, f32[1536,128]{1,0:T(8,128)S(1)} %shard_map.113.base, f32[6,128,128]{2,1,0:T(8,128)S(1)} %bitcast.12, ...), custom_call_target="tpu_custom_call" | custom-call | tf_op jit(solution)/shard_map/pallas_call | solution.py:289
  109.1 5.4 %all-to-all-start.1 = ((f32[8,128,128]{2,1,0:T(8,128)}), f32[8,128,128]{2,1,0:T(8,128)}, u32[]{:S(2)}, u32[]{:S(2)}) async-start(f32[8,128,128]{2,1,0:T(8,128)} %get-tuple-element.48), calls=%async_computation.1 | async-start | bytes 1048576 | tf_op jit(solution)/shard_map/all_to_all | solution.py:389
  117.7 4.2 %shard_map.120 = (f32[8,128,128]{2,1,0:T(8,128)S(1)}, f32[1536,128]{1,0:T(8,128)S(1)}) custom-call(s32[6]{0:T(128)S(1)} %bitcast.20, s32[8]{0:T(128)S(1)} %bitcast.28, s32[1]{0:T(128)} %bitcast.9.first_ref, f32[1,1024]{1,0:T(1,128)S(1)} %bitcast.24, f32[1536,128]{1,0:T(8,128)S(1)} %copy-done.29, f32[6,128,128]{2,1,0:T(8,128)S(1)} %bitcast.13, ...), custom_call_target="tpu_custom_call" | custom-call | flops 49999998976 | tf_op jit(solution)/shard_map/pallas_call | solution.py:289
  123.7 5.4 %all-to-all-done.1.incoming = f32[8,128,128]{2,1,0:T(8,128)} async-done(((f32[8,128,128]{2,1,0:T(8,128)}), f32[8,128,128]{2,1,0:T(8,128)}, u32[]{:S(2)}, u32[]{:S(2)}) %all-to-all-start.1) | async-done | bytes 524320 | tf_op jit(solution)/shard_map/all_to_all | solution.py:389
  129.0 4.3 %all-to-all-start.2 = ((f32[8,128,128]{2,1,0:T(8,128)}), f32[8,128,128]{2,1,0:T(8,128)}, u32[]{:S(2)}, u32[]{:S(2)}) async-start(f32[8,128,128]{2,1,0:T(8,128)} %copy-done.19), calls=%async_computation.2 | async-start | bytes 1048576 | tf_op jit(solution)/shard_map/all_to_all | solution.py:389
  133.4 3.2 %shard_map.118 = (f32[384,128]{1,0:T(8,128)S(1)}, f32[384,128]{1,0:T(8,128)S(1)}, f32[384,128]{1,0:T(8,128)}, f32[384,128]{1,0:T(8,128)S(1)}) custom-call(s32[6]{0:T(128)S(1)} %bitcast.17, s32[6]{0:T(128)S(1)} %bitcast.21, s32[4]{0:T(128)S(1)} %pad_add_fusion.place_ref, f32[1536,128]{1,0:T(8,128)S(1)} %copy-done.18, f32[6,128,128]{2,1,0:T(8,128)S(1)} %bitcast.14, ...), custom_call_target="tpu_custom_call" | custom-call | tf_op jit(solution)/shard_map/pallas_call | solution.py:321
  136.7 1.6 collective-permute-start.11
  138.6 8.9 %all-to-all-done.2.incoming = f32[8,128,128]{2,1,0:T(8,128)} async-done(((f32[8,128,128]{2,1,0:T(8,128)}), f32[8,128,128]{2,1,0:T(8,128)}, u32[]{:S(2)}, u32[]{:S(2)}) %all-to-all-start.2) | async-done | bytes 524320 | tf_op jit(solution)/shard_map/all_to_all | solution.py:389
  148.6 3.1 %shard_map.121 = (f32[384,128]{1,0:T(8,128)S(1)}, f32[384,128]{1,0:T(8,128)S(1)}, f32[384,128]{1,0:T(8,128)S(1)}, f32[384,128]{1,0:T(8,128)S(1)}) custom-call(s32[6]{0:T(128)S(1)} %bitcast.18, s32[6]{0:T(128)S(1)} %bitcast.22, s32[4]{0:T(128)S(1)} %pad_add_fusion.place_ref, f32[1536,128]{1,0:T(8,128)S(1)} %copy-done.16, f32[6,128,128]{2,1,0:T(8,128)S(1)} %bitcast.15, ...), custom_call_target="tpu_custom_call" | custom-call | tf_op jit(solution)/shard_map/pallas_call | solution.py:321
  151.7 1.6 collective-permute-start.15
  154.7 4.2 %shard_map.119.start = f32[384,1024]{1,0:T(8,128)S(1)} custom-call(s32[1]{0:T(128)S(6)} %select_n.60.turn_ref, f32[1,1024]{1,0:T(1,128)S(1)} %bitcast.25, f32[384,128]{1,0:T(8,128)S(1)} %get-tuple-element.49.refs_0_, f32[384,128]{1,0:T(8,128)} %collective-permute-done.10.refs_1_, f32[384,128]{1,0:T(8,128)} %collective-permute-done.11.refs_2_, ...), custom_call_target="tpu_custom_call" | custom-call | flops 1207959552 | tf_op jit(solution)/shard_map/pallas_call | solution.py:358
  159.5 3.3 %collective-permute-done.16.refs_3_ = f32[384,128]{1,0:T(8,128)S(1)} collective-permute-done((f32[384,128]{1,0:T(8,128)S(1)}, f32[384,128]{1,0:T(8,128)S(1)}, u32[]{:S(2)}, u32[]{:S(2)}) %collective-permute-start.16) | collective-permute-done | bytes 196640 | tf_op jit(solution)/shard_map/ppermute | solution.py:386
  162.8 4.9 %shard_map.122 = f32[384,1024]{1,0:T(8,128)} custom-call(s32[1]{0:T(128)S(6)} %select_n.59.turn_ref, f32[384,1024]{1,0:T(8,128)S(1)} %shard_map.119.start, f32[384,128]{1,0:T(8,128)S(1)} %get-tuple-element.65.refs_0_, f32[384,128]{1,0:T(8,128)S(1)} %collective-permute-done.14.refs_1_, f32[384,128]{1,0:T(8,128)S(1)} %collective-permute-done.15.refs_2_, ...), custom_call_target="tpu_custom_call" | custom-call | flops 1207959552 | tf_op jit(solution)/shard_map/pallas_call | solution.py:358
  (89 shorter events, 19.6 us)
Async XLA Ops:
  0.0 34.9 %collective-permute-start = (f32[1536,256]{1,0:T(8,128)}, f32[1536,256]{1,0:T(8,128)}, u32[]{:S(2)}, u32[]{:S(2)}) collective-permute-start(f32[1536,256]{1,0:T(8,128)} %refs_0_.1), channel_id=1, source_target_pairs={{0,1},{1,0},{2,3},{3,2},{4,5},{5,4},{6,7},{7,6},{8,9},{9,8},{10,11... | collective-permute-start | bytes 4718600 | tf_op jit(solution)/shard_map/ppermute | solution.py:386
  0.5 34.4 %collective-permute-start.1 = (f32[256,1024]{1,0:T(8,128)}, f32[256,1024]{1,0:T(8,128)S(1)}, u32[]{:S(2)}, u32[]{:S(2)}) collective-permute-start(f32[256,1024]{1,0:T(8,128)} %refs_2_.7), channel_id=1, source_target_pairs={{0,1},{1,0},{2,3},{3,2},{4,5},{5,4},{6,7},{7,6},{8,9},{9,8},{10,11... | collective-permute-start | bytes 3145736 | tf_op jit(solution)/shard_map/ppermute | solution.py:386
  8.8 26.1 %copy-start = (f32[256,1024]{1,0:T(8,128)S(1)}, f32[256,1024]{1,0:T(8,128)}, u32[]{:S(2)}) copy-start(f32[256,1024]{1,0:T(8,128)} %refs_2_.7) | copy-start | bytes 3145732
  8.8 59.0 %all-to-all-start = ((f32[8,128,256]{2,1,0:T(8,128)}), f32[8,128,256]{2,1,0:T(8,128)}, u32[]{:S(2)}, u32[]{:S(2)}) async-start(f32[8,128,256]{2,1,0:T(8,128)} %copy-done.3), calls=%async_computation | async-start | bytes 2097152 | tf_op jit(solution)/shard_map/all_to_all | solution.py:389
  33.2 13.8 %collective-permute-start.3 = (f32[128,1024]{1,0:T(8,128)}, f32[128,1024]{1,0:T(8,128)S(1)}, u32[]{:S(2)}, u32[]{:S(2)}) collective-permute-start(f32[128,1024]{1,0:T(8,128)} %shard_map.111), channel_id=1, source_target_pairs={{0,2},{1,3},{2,0},{3,1},{4,6},{5,7},{6,4},{7,5},{8,10},{9,11},{10,... | collective-permute-start | bytes 1572872 | tf_op jit(solution)/shard_map/ppermute | solution.py:386
  34.8 33.0 %collective-permute-start.2 = (f32[256,1024]{1,0:T(8,128)}, f32[256,1024]{1,0:T(8,128)}, u32[]{:S(2)}, u32[]{:S(2)}) collective-permute-start(f32[256,1024]{1,0:T(8,128)} %refs_4_.1), channel_id=1, source_target_pairs={{0,1},{1,0},{2,3},{3,2},{4,5},{5,4},{6,7},{7,6},{8,9},{9,8},{10,11... | collective-permute-start | bytes 3145736 | tf_op jit(solution)/shard_map/ppermute | solution.py:386
  47.0 19.0 %copy-start.9 = (f32[128,1024]{1,0:T(8,128)}, f32[128,1024]{1,0:T(8,128)S(1)}, u32[]{:S(2)}) copy-start(f32[128,1024]{1,0:T(8,128)S(1)} %collective-permute-done.3.refs_6_) | copy-start | bytes 1572868
  47.0 20.8 %copy-start.22 = (s32[1,6]{1,0:T(1,128)S(1)}, s32[1,6]{1,0:T(1,128)}, u32[]{:S(2)}) copy-start(s32[1,6]{1,0:T(1,128)} %param.16) | copy-start | bytes 76
  47.0 12.8 %collective-permute-start.4 = (f32[128,1024]{1,0:T(8,128)S(1)}, f32[128,1024]{1,0:T(8,128)}, u32[]{:S(2)}, u32[]{:S(2)}) collective-permute-start(f32[128,1024]{1,0:T(8,128)S(1)} %collective-permute-done.3.refs_6_), channel_id=1, source_target_pairs={{0,4},{4,0},{8,12},{12,8},{16,20},{20,16},{24,28},{28,24},{1,5},{5... | collective-permute-start | bytes 1572872 | tf_op jit(solution)/shard_map/ppermute | solution.py:426
  48.8 19.1 %collective-permute-start.5 = (f32[128,1024]{1,0:T(8,128)S(1)}, f32[128,1024]{1,0:T(8,128)}, u32[]{:S(2)}, u32[]{:S(2)}) collective-permute-start(f32[128,1024]{1,0:T(8,128)S(1)} %collective-permute-done.3.refs_6_), channel_id=1, source_target_pairs={{0,1},{1,0},{2,3},{3,2},{4,5},{5,4},{6,7},{7,6},{8,9},{9,8},{10,11... | collective-permute-start | bytes 1572872 | tf_op jit(solution)/shard_map/ppermute | solution.py:386
  59.8 8.1 %collective-permute-start.6 = (f32[128,1024]{1,0:T(8,128)}, f32[128,1024]{1,0:T(8,128)}, u32[]{:S(2)}, u32[]{:S(2)}) collective-permute-start(f32[128,1024]{1,0:T(8,128)} %collective-permute-done.4.refs_7_), channel_id=1, source_target_pairs={{0,1},{1,0},{2,3},{3,2},{4,5},{5,4},{6,7},{7,6},{8,9},{9,8},{10,11... | collective-permute-start | bytes 1572872 | tf_op jit(solution)/shard_map/ppermute | solution.py:386
  59.8 27.7 %collective-permute-start.7 = (f32[2176,128]{1,0:T(8,128)}, f32[2176,128]{1,0:T(8,128)}, u32[]{:S(2)}, u32[]{:S(2)}) collective-permute-start(f32[2176,128]{1,0:T(8,128)} %get-tuple-element.40), channel_id=1, source_target_pairs={{0,2},{1,3},{2,0},{3,1},{4,6},{5,7},{6,4},{7,5},{8,10},{9,11},{10,... | collective-permute-start | bytes 3342344 | tf_op jit(solution)/shard_map/ppermute | solution.py:386
  69.5 3.9 %copy-start.5 = (f32[384,256]{1,0:T(8,128)}, f32[384,256]{1,0:T(8,128)S(1)}, u32[]{:S(2)}) copy-start(f32[384,256]{1,0:T(8,128)S(1)} %shard_map.114.refs_0_) | copy-start | bytes 1179652
  69.5 1.8 %collective-permute-start.8 = (f32[384,256]{1,0:T(8,128)S(1)}, f32[384,256]{1,0:T(8,128)S(1)}, u32[]{:S(2)}, u32[]{:S(2)}) collective-permute-start(f32[384,256]{1,0:T(8,128)S(1)} %shard_map.114.refs_0_), channel_id=1, source_target_pairs={{0,1},{1,0},{2,3},{3,2},{4,5},{5,4},{6,7},{7,6},{8,9},{9,8},{10,11... | collective-permute-start | bytes 1179656 | tf_op jit(solution)/shard_map/ppermute | solution.py:386
  73.4 41.2 %collective-permute-start.13 = (f32[1280,128]{1,0:T(8,128)}, f32[1280,128]{1,0:T(8,128)}, u32[]{:S(2)}, u32[]{:S(2)}) collective-permute-start(f32[1280,128]{1,0:T(8,128)} %get-tuple-element.62), channel_id=1, source_target_pairs={{0,2},{1,3},{2,0},{3,1},{4,6},{5,7},{6,4},{7,5},{8,10},{9,11},{10,... | collective-permute-start | bytes 1966088 | tf_op jit(solution)/shard_map/ppermute | solution.py:386
  73.9 31.3 %collective-permute-start.9 = (f32[384,128]{1,0:T(8,128)}, f32[384,128]{1,0:T(8,128)S(1)}, u32[]{:S(2)}, u32[]{:S(2)}) collective-permute-start(f32[384,128]{1,0:T(8,128)} %get-tuple-element.46), channel_id=1, source_target_pairs={{0,2},{1,3},{2,0},{3,1},{4,6},{5,7},{6,4},{7,5},{8,10},{9,11},{10,... | collective-permute-start | bytes 589832 | tf_op jit(solution)/shard_map/ppermute | solution.py:386
  75.5 16.2 %copy-start.6 = (f32[384,256]{1,0:T(8,128)S(1)}, f32[384,256]{1,0:T(8,128)}, u32[]{:S(2)}) copy-start(f32[384,256]{1,0:T(8,128)} %copy-done.5) | copy-start | bytes 1179652
  91.6 13.6 %copy-start.4 = (f32[1,6,128,128]{3,2,1,0:T(8,128)S(1)}, f32[1,6,128,128]{3,2,1,0:T(8,128)}, u32[]{:S(2)}) copy-start(f32[1,6,128,128]{3,2,1,0:T(8,128)} %param.14) | copy-start | bytes 1179652
  91.7 13.6 %copy-start.23 = (s32[1,6]{1,0:T(1,128)S(1)}, s32[1,6]{1,0:T(1,128)}, u32[]{:S(2)}) copy-start(s32[1,6]{1,0:T(1,128)} %param.17) | copy-start | bytes 76
  91.7 13.6 %copy-start.24 = (f32[1024]{0:T(1024)S(1)}, f32[1024]{0:T(1024)}, u32[]{:S(2)}) copy-start(f32[1024]{0:T(1024)} %param.19) | copy-start | bytes 12292
  91.7 13.6 %copy-start.27 = (s32[1,8]{1,0:T(1,128)S(1)}, s32[1,8]{1,0:T(1,128)}, u32[]{:S(2)}) copy-start(s32[1,8]{1,0:T(1,128)} %param.15) | copy-start | bytes 100
  93.0 15.2 %copy-start.30 = (f32[384,128]{1,0:T(8,128)}, f32[384,128]{1,0:T(8,128)S(1)}, u32[]{:S(2)}) copy-start(f32[384,128]{1,0:T(8,128)S(1)} %get-tuple-element.61.refs_0_) | copy-start | bytes 589828
  109.1 19.9 %all-to-all-start.1 = ((f32[8,128,128]{2,1,0:T(8,128)}), f32[8,128,128]{2,1,0:T(8,128)}, u32[]{:S(2)}, u32[]{:S(2)}) async-start(f32[8,128,128]{2,1,0:T(8,128)} %get-tuple-element.48), calls=%async_computation.1 | async-start | bytes 1048576 | tf_op jit(solution)/shard_map/all_to_all | solution.py:389
  123.7 9.7 %copy-start.18 = (f32[1536,128]{1,0:T(8,128)S(1)}, f32[1536,128]{1,0:T(8,128)}, u32[]{:S(2)}) copy-start(f32[1536,128]{1,0:T(8,128)} %copy-done.17) | copy-start | bytes 2359300
  129.0 18.4 %all-to-all-start.2 = ((f32[8,128,128]{2,1,0:T(8,128)}), f32[8,128,128]{2,1,0:T(8,128)}, u32[]{:S(2)}, u32[]{:S(2)}) async-start(f32[8,128,128]{2,1,0:T(8,128)} %copy-done.19), calls=%async_computation.2 | async-start | bytes 1048576 | tf_op jit(solution)/shard_map/all_to_all | solution.py:389
  136.6 17.0 %copy-start.25 = (f32[1024]{0:T(1024)S(1)}, f32[1024]{0:T(1024)}, u32[]{:S(2)}) copy-start(f32[1024]{0:T(1024)} %param.21) | copy-start | bytes 12292
  136.6 16.7 %collective-permute-start.10 = (f32[384,128]{1,0:T(8,128)S(1)}, f32[384,128]{1,0:T(8,128)}, u32[]{:S(2)}, u32[]{:S(2)}) collective-permute-start(f32[384,128]{1,0:T(8,128)S(1)} %get-tuple-element.50), channel_id=1, source_target_pairs={{0,1},{1,0},{2,3},{3,2},{4,5},{5,4},{6,7},{7,6},{8,9},{9,8},{10,11... | collective-permute-start | bytes 589832 | tf_op jit(solution)/shard_map/ppermute | solution.py:386
  136.7 16.9 %collective-permute-start.11 = (f32[384,128]{1,0:T(8,128)}, f32[384,128]{1,0:T(8,128)}, u32[]{:S(2)}, u32[]{:S(2)}) collective-permute-start(f32[384,128]{1,0:T(8,128)} %get-tuple-element.51), channel_id=1, source_target_pairs={{0,2},{1,3},{2,0},{3,1},{4,6},{5,7},{6,4},{7,5},{8,10},{9,11},{10,... | collective-permute-start | bytes 589832 | tf_op jit(solution)/shard_map/ppermute | solution.py:386
  138.3 15.3 %collective-permute-start.12 = (f32[384,128]{1,0:T(8,128)S(1)}, f32[384,128]{1,0:T(8,128)}, u32[]{:S(2)}, u32[]{:S(2)}) collective-permute-start(f32[384,128]{1,0:T(8,128)S(1)} %get-tuple-element.52), channel_id=1, source_target_pairs={{0,3},{1,2},{2,1},{3,0},{4,7},{5,6},{6,5},{7,4},{8,11},{9,10},{10,... | collective-permute-start | bytes 589832 | tf_op jit(solution)/shard_map/ppermute | solution.py:386
  151.7 7.2 %collective-permute-start.14 = (f32[384,128]{1,0:T(8,128)S(1)}, f32[384,128]{1,0:T(8,128)S(1)}, u32[]{:S(2)}, u32[]{:S(2)}) collective-permute-start(f32[384,128]{1,0:T(8,128)S(1)} %get-tuple-element.66), channel_id=1, source_target_pairs={{0,1},{1,0},{2,3},{3,2},{4,5},{5,4},{6,7},{7,6},{8,9},{9,8},{10,11... | collective-permute-start | bytes 589832 | tf_op jit(solution)/shard_map/ppermute | solution.py:386
  151.7 7.8 %collective-permute-start.15 = (f32[384,128]{1,0:T(8,128)S(1)}, f32[384,128]{1,0:T(8,128)S(1)}, u32[]{:S(2)}, u32[]{:S(2)}) collective-permute-start(f32[384,128]{1,0:T(8,128)S(1)} %get-tuple-element.67), channel_id=1, source_target_pairs={{0,2},{1,3},{2,0},{3,1},{4,6},{5,7},{6,4},{7,5},{8,10},{9,11},{10,... | collective-permute-start | bytes 589832 | tf_op jit(solution)/shard_map/ppermute | solution.py:386
  153.3 9.5 %collective-permute-start.16 = (f32[384,128]{1,0:T(8,128)S(1)}, f32[384,128]{1,0:T(8,128)S(1)}, u32[]{:S(2)}, u32[]{:S(2)}) collective-permute-start(f32[384,128]{1,0:T(8,128)S(1)} %get-tuple-element.68), channel_id=1, source_target_pairs={{0,3},{1,2},{2,1},{3,0},{4,7},{5,6},{6,5},{7,4},{8,11},{9,10},{10,... | collective-permute-start | bytes 589832 | tf_op jit(solution)/shard_map/ppermute | solution.py:386
  (20 other events, 24.8 us)
